TPU v7x, 512 devices: a whole 4x8x8 slice. The times are simulated.
512 devices in a mesh: member: 32 (over z_lo, y, core), space: 16 (over x, z_hi).
Axes of the slice: x: 4, y: 8, z: 8 (z_hi: 4, z_lo: 2; z = z_hi * 2 + z_lo), core: 2. Of those that a mesh axis runs over, the one named last changes fastest.
Arguments:
- participant_swirls: float32 [64, 512, 512], P('member', 'space'), may hold values from -6 to 6
- driving_source: float32 [512, 512], P('space'), may hold values from -12 to 12
- mixing: float32 [64, 64], replicated, may hold values from -0.75 to 0.75
- probes: int32 [32768], P('space'), may hold values from 0 to 16383
- observed: float32 [32768], P('space'), may hold values from -6 to 6
Outputs:
- analysis: float32 [64, 512, 512], P('member', 'space')
- spread: float32 [64, 64], replicated
- projection: float32 [64], replicated
Inputs may be any that keep to these rules, and one draw needn't show every extreme that they name: `probes`: each index names a cell of its own block's 32 rows, row-major with 512 columns.
All inputs are finite; a program needn't handle non-finite values.
Results may differ from a plain program's by a relative error of at most 0.0003.
Values may be sent and summed in bfloat16 or wider, within the bound.
A program may use at most 64 MiB of HBM per device.

v0:
```python
import math

import jax
import jax.numpy as jnp
from jax import lax
from jax.sharding import PartitionSpec as P

N = 512
KEEP = 160


DT_STEP = 0.1
VISCOSITY = 0.05
EXACT = lax.Precision.HIGHEST


def copy_for_each(value, axis):
    peers = lax.axis_size(axis)
    return lax.all_to_all(
        jnp.broadcast_to(value[None], (peers, *value.shape)), axis, 0, 0, tiled=True
    )


def in_order(blocks, dim):
    blocks = jnp.moveaxis(blocks, 0, dim)
    dims = blocks.shape
    return blocks.reshape(*dims[:dim], dims[dim] * dims[dim + 1], *dims[dim + 2 :])


def gather_directly(value, axis, dim):
    blocks = copy_for_each(value, axis)
    return in_order(blocks, dim)


def of_everyone(value, axis):
    return copy_for_each(value, axis).sum(axis=0)


def together(arrays, axis):
    ends = [0]
    for a in arrays:
        ends.append(ends[-1] + a.size)
    subtotal = of_everyone(jnp.concatenate([a.ravel() for a in arrays]), axis)
    return tuple((subtotal[b:e].reshape(a.shape) for a, b, e in zip(arrays, ends, ends[1:])))


def phase_tables(positions, numbers):
    turns = positions[:, None] * numbers[None, :] % N
    angles = turns.astype(jnp.float32) * (2.0 * math.pi / N)
    return (jnp.cos(angles), jnp.sin(angles))


def signed_slots():
    slots = jnp.arange(2 * KEEP, dtype=jnp.int32)
    return jnp.where(slots < KEEP, slots, slots - 2 * KEEP)


def all_tables():
    cells = jnp.arange(N, dtype=jnp.int32)
    cos_y, sin_y = phase_tables(cells, jnp.arange(KEEP, dtype=jnp.int32))
    cos_x, sin_x = phase_tables(cells, signed_slots())
    return (cos_y, sin_y, cos_x, sin_x)


def rows_to_modes(field, precomputed_trig):
    real_part = jnp.einsum("brn,nk->bkr", field, precomputed_trig[0], precision=EXACT)
    imag_part = -jnp.einsum("brn,nk->bkr", field, precomputed_trig[1], precision=EXACT)
    stacked = jnp.stack([real_part, imag_part], 1)
    moved = lax.all_to_all(stacked, "space", split_axis=2, concat_axis=3, tiled=True)
    with_cos = jnp.einsum("bpkn,nq->bpkq", moved, precomputed_trig[2], precision=EXACT)
    with_sin = jnp.einsum("bpkn,nq->bpkq", moved, precomputed_trig[3], precision=EXACT)
    factor = 1.0 / (N * N)
    return ((with_cos[:, 0] + with_sin[:, 1]) * factor, (with_cos[:, 1] - with_sin[:, 0]) * factor)


def modes_to_columns(real_part, imag_part, precomputed_trig):
    stacked = jnp.stack([real_part, imag_part], 1)
    with_cos = jnp.einsum("bpkq,nq->bpkn", stacked, precomputed_trig[2], precision=EXACT)
    with_sin = jnp.einsum("bpkq,nq->bpkn", stacked, precomputed_trig[3], precision=EXACT)
    return jnp.stack([with_cos[:, 0] - with_sin[:, 1], with_sin[:, 0] + with_cos[:, 1]], 1)


def columns_to_rows(moved, precomputed_trig):
    counts = jnp.where(jnp.arange(KEEP) == 0, 1.0, 2.0).astype(jnp.float32)[None, :, None]
    cosine = jnp.einsum("bkr,nk->brn", moved[:, 0] * counts, precomputed_trig[0], precision=EXACT)
    sine = jnp.einsum("bkr,nk->brn", moved[:, 1] * counts, precomputed_trig[1], precision=EXACT)
    return cosine - sine


def advance_model_once(participant_swirls, driving_source, precomputed_trig):
    count = participant_swirls.shape[0]
    width = KEEP // lax.axis_size("space")
    scale = 2.0 * math.pi / N
    first = lax.axis_index("space") * width + jnp.arange(width, dtype=jnp.int32)
    wave_y = (first.astype(jnp.float32) * scale)[:, None]
    wave_x = (signed_slots().astype(jnp.float32) * scale)[None, :]
    squared = wave_x * wave_x + wave_y * wave_y
    inverse_sq = jnp.where(squared > 0, 1.0 / jnp.where(squared > 0, squared, 1.0), 0.0)
    vort_re, vort_im = rows_to_modes(participant_swirls, precomputed_trig)
    stream_re = vort_re * inverse_sq
    stream_im = vort_im * inverse_sq
    fields_re = jnp.concatenate(
        [-wave_y * stream_im, wave_x * stream_im, -wave_x * vort_im, -wave_y * vort_im], 0
    )
    fields_im = jnp.concatenate(
        [wave_y * stream_re, -wave_x * stream_re, wave_x * vort_re, wave_y * vort_re], 0
    )
    columns = modes_to_columns(fields_re, fields_im, precomputed_trig)
    moved = lax.all_to_all(columns, "space", split_axis=3, concat_axis=2, tiled=True)
    physical = columns_to_rows(moved, precomputed_trig)
    vel_x = physical[:count]
    vel_y = physical[count : 2 * count]
    grad_x = physical[2 * count : 3 * count]
    grad_y = physical[3 * count :]
    advect = vel_x * grad_x + vel_y * grad_y
    adv_re, adv_im = rows_to_modes(advect, precomputed_trig)
    new_re = vort_re + DT_STEP * (-adv_re - VISCOSITY * squared * vort_re)
    new_im = vort_im + DT_STEP * (-adv_im - VISCOSITY * squared * vort_im)
    columns = modes_to_columns(new_re, new_im, precomputed_trig)
    moved = lax.all_to_all(columns, "space", split_axis=3, concat_axis=2, tiled=True)
    return columns_to_rows(moved, precomputed_trig) + DT_STEP * driving_source[None]


def on_device(participant_swirls, driving_source, mixing, probes, observed):
    precomputed_trig = all_tables()
    count_local = participant_swirls.shape[0]
    random_perturbations = advance_model_once(participant_swirls, driving_source, precomputed_trig)
    rounded = random_perturbations.astype(jnp.bfloat16)
    values = lax.all_to_all(rounded, "member", split_axis=1, concat_axis=0, tiled=True).astype(
        jnp.float32
    )
    centre_rows = jnp.mean(values, 0)
    mixed = jnp.einsum("jrn,jm->mrn", values, mixing, precision=EXACT)
    mixed = mixed + (1.0 - jnp.sum(mixing, 0))[:, None, None] * centre_rows[None]
    analysis = lax.all_to_all(mixed, "member", split_axis=0, concat_axis=1, tiled=True)
    flat = rounded.reshape(count_local, -1)
    picked = jnp.take(flat, probes, axis=1)
    everyone = gather_directly(picked, "member", 0).astype(jnp.float32)
    centre = jnp.mean(everyone, 0)
    anomaly = everyone - centre[None]
    local_spread = jnp.dot(anomaly, anomaly.T, precision=EXACT)
    local_proj = jnp.dot(anomaly, observed - centre, precision=EXACT)
    spread, projection = together((local_spread, local_proj), "space")
    total_probes = probes.shape[0] * lax.axis_size("space")
    return (analysis, spread / total_probes, projection / math.sqrt(total_probes))


def solution(mesh):
    return jax.shard_map(
        on_device,
        mesh=mesh,
        in_specs=(P("member", "space", None), P("space", None), P(), P("space"), P("space")),
        out_specs=(P("member", "space", None), P(), P()),
        check_vma=False,
    )
```

profile of v0, /device:TPU:1, one launch (start us, length us, event | category | flops | bytes accessed | tf_op | source)
XLA Modules:
  0.0 228.2 jit_solution(793400455002237478)
XLA Ops:
  6.1 13.6 %all-to-all-start = ((f32[16,1,1280]{2,1,0:T(1,128)}), f32[16,1,1280]{2,1,0:T(1,128)S(1)}, u32[]{:S(2)}, u32[]{:S(2)}) async-start(f32[16,1,1280]{2,1,0:T(1,128)} %reshape.229), calls=%async_computation | async-start | bytes 163840 | tf_op jit(solution)/shard_map/all_to_all | solution.py:69
  19.9 9.0 %all-to-all-done = f32[16,1,1280]{2,1,0:T(1,128)S(1)} async-done(((f32[16,1,1280]{2,1,0:T(1,128)}), f32[16,1,1280]{2,1,0:T(1,128)S(1)}, u32[]{:S(2)}, u32[]{:S(2)}) %all-to-all-start) | async-done | bytes 81952 | tf_op jit(solution)/shard_map/all_to_all | solution.py:69
  30.8 3.1 %fusion.17 = f32[2,2,10,320]{3,2,1,0:T(8,128)S(1)} fusion(f32[2,2,10,512]{3,2,1,0:T(8,128)S(1)} %reshape.227, s32[320]{0:T(512)S(1)} %compare_select_fusion.1), kind=kOutput, calls=%fused_computation.31 | convolution fusion | flops 80936960 | bytes 134400 | tf_op jit(solution)/shard_map/bpkn,nq->bpkq/dot_general | solution.py:71
  33.9 3.1 %fusion.25 = f32[2,2,10,320]{3,2,1,0:T(8,128)S(1)} fusion(f32[2,2,10,512]{3,2,1,0:T(8,128)S(1)} %reshape.227, s32[320]{0:T(512)S(1)} %compare_select_fusion.1), kind=kOutput, calls=%fused_computation.39 | convolution fusion | flops 80936960 | bytes 134400 | tf_op jit(solution)/shard_map/bpkn,nq->bpkq/dot_general | solution.py:70
  37.2 3.5 %fusion.23 = f32[8,2,10,512]{3,2,1,0:T(8,128)S(1)} fusion(s32[320]{0:T(512)S(1)} %compare_select_fusion.1, f32[8,1,10,320]{3,2,0,1:T(8,128)S(1)} %maximum_bitcast_fusion.1, f32[8,1,10,320]{3,2,0,1:T(8,128)S(1)} %maximum_bitcast_fusion), kind=kOutput, calls=%fused_computation.37 | convolution fusion | flops 316917760 | bytes 533760 | tf_op jit(solution)/shard_map/bpkq,nq->bpkn/dot_general | solution.py:78
  40.7 3.9 %fusion.15 = f32[8,2,10,512]{3,2,1,0:T(8,128)S(1)} fusion(s32[320]{0:T(512)S(1)} %compare_select_fusion.1, f32[8,1,10,320]{3,2,0,1:T(8,128)S(1)} %maximum_bitcast_fusion.1, f32[8,1,10,320]{3,2,0,1:T(8,128)S(1)} %maximum_bitcast_fusion), kind=kOutput, calls=%fused_computation.29 | convolution fusion | flops 316917760 | bytes 533760 | tf_op jit(solution)/shard_map/bpkq,nq->bpkn/dot_general | solution.py:79
  44.8 4.5 %copy.132 = f32[8,2,10,512]{2,1,0,3:T(2,128)} copy(f32[8,2,10,512]{3,2,1,0:T(8,128)S(1)} %pad_maximum_fusion) | data formatting | bytes 655360 | tf_op jit(solution)/shard_map/stack | solution.py:80
  49.3 8.8 %reshape.231 = f32[16,1,5120]{2,1,0:T(1,128)} reshape(f32[512,8,2,10]{3,2,1,0:T(2,128)} %bitcast.153) | data formatting | bytes 655360
  58.1 3.5 %all-to-all-start.1 = ((f32[16,1,5120]{2,1,0:T(1,128)}), f32[16,1,5120]{2,1,0:T(1,128)S(1)}, u32[]{:S(2)}, u32[]{:S(2)}) async-start(f32[16,1,5120]{2,1,0:T(1,128)} %reshape.231), calls=%async_computation.1 | async-start | bytes 655360 | tf_op jit(solution)/shard_map/all_to_all | solution.py:109
  61.7 12.6 %all-to-all-done.1 = f32[16,1,5120]{2,1,0:T(1,128)S(1)} async-done(((f32[16,1,5120]{2,1,0:T(1,128)}), f32[16,1,5120]{2,1,0:T(1,128)S(1)}, u32[]{:S(2)}, u32[]{:S(2)}) %all-to-all-start.1) | async-done | bytes 327712 | tf_op jit(solution)/shard_map/all_to_all | solution.py:109
  75.7 8.0 %reshape.232 = f32[512,8,2,10]{3,2,1,0:T(2,128)} reshape(f32[16,5120]{1,0:T(8,128)S(1)} %reduce.5) | data formatting | bytes 655360
  83.6 5.7 %copy.161 = f32[8,2,10,16,32]{4,0,2,3,1:T(8,128)S(1)} copy(f32[8,2,10,16,32]{2,1,0,4,3:T(2,128)} %bitcast.154) | data formatting | bytes 655360 | tf_op jit(solution)/shard_map/all_to_all | solution.py:109
  89.7 2.3 %fusion.28 = f32[8,32,512]{2,1,0:T(8,128)S(1)} fusion(f32[8,160,32]{2,0,1:T(8,128)S(1)} %get-tuple-element.8), kind=kOutput, calls=%fused_computation.42 | convolution fusion | flops 252805120 | bytes 688128 | tf_op jit(solution)/shard_map/bkr,nk->brn/dot_general | solution.py:85
  91.9 2.3 %convolution_subtract_fusion = f32[8,32,512]{2,1,0:T(8,128)S(1)} fusion(f32[8,32,512]{2,1,0:T(8,128)S(1)} %fusion.28, f32[8,160,32]{2,0,1:T(8,128)S(1)} %get-tuple-element.7), kind=kOutput, calls=%fused_computation.1 | convolution fusion | flops 252936192 | bytes 1212416 | tf_op jit(solution)/shard_map/bkr,nk->brn/dot_general | solution.py:86
  98.8 3.7 %all-to-all-start.2 = ((f32[16,1,1280]{2,1,0:T(1,128)}), f32[16,1,1280]{2,1,0:T(1,128)S(1)}, u32[]{:S(2)}, u32[]{:S(2)}) async-start(f32[16,1,1280]{2,1,0:T(1,128)} %reshape.233), calls=%async_computation.2 | async-start | bytes 163840 | tf_op jit(solution)/shard_map/all_to_all | solution.py:69
  102.6 9.0 %all-to-all-done.2 = f32[16,1,1280]{2,1,0:T(1,128)S(1)} async-done(((f32[16,1,1280]{2,1,0:T(1,128)}), f32[16,1,1280]{2,1,0:T(1,128)S(1)}, u32[]{:S(2)}, u32[]{:S(2)}) %all-to-all-start.2) | async-done | bytes 81952 | tf_op jit(solution)/shard_map/all_to_all | solution.py:69
  112.9 3.1 %fusion.21 = f32[2,2,10,320]{3,2,1,0:T(8,128)S(1)} fusion(f32[2,2,10,512]{3,2,1,0:T(8,128)S(1)} %reshape.228, s32[320]{0:T(512)S(1)} %compare_select_fusion.1), kind=kOutput, calls=%fused_computation.35 | convolution fusion | flops 80936960 | bytes 134400 | tf_op jit(solution)/shard_map/bpkn,nq->bpkq/dot_general | solution.py:70
  116.0 3.1 %fusion.13 = f32[2,2,10,320]{3,2,1,0:T(8,128)S(1)} fusion(f32[2,2,10,512]{3,2,1,0:T(8,128)S(1)} %reshape.228, s32[320]{0:T(512)S(1)} %compare_select_fusion.1), kind=kOutput, calls=%fused_computation.27 | convolution fusion | flops 80936960 | bytes 134400 | tf_op jit(solution)/shard_map/bpkn,nq->bpkq/dot_general | solution.py:71
  119.2 3.0 %fusion.19 = f32[2,2,10,512]{3,2,1,0:T(8,128)S(1)} fusion(s32[320]{0:T(512)S(1)} %compare_select_fusion.1, f32[2,1,10,320]{3,2,1,0:T(8,128)S(1)} %get-tuple-element.16, f32[2,1,10,320]{3,2,1,0:T(8,128)S(1)} %get-tuple-element.15), kind=kOutput, calls=%fused_computation.33 | convolution fusion | flops 80949760 | bytes 134400 | tf_op jit(solution)/shard_map/bpkq,nq->bpkn/dot_general | solution.py:78
  122.2 3.2 %fusion.11 = f32[2,2,10,512]{3,2,1,0:T(8,128)S(1)} fusion(s32[320]{0:T(512)S(1)} %compare_select_fusion.1, f32[2,1,10,320]{3,2,1,0:T(8,128)S(1)} %get-tuple-element.16, f32[2,1,10,320]{3,2,1,0:T(8,128)S(1)} %get-tuple-element.15), kind=kOutput, calls=%fused_computation.25 | convolution fusion | flops 80949760 | bytes 134400 | tf_op jit(solution)/shard_map/bpkq,nq->bpkn/dot_general | solution.py:79
  126.2 2.2 reshape.235
  128.4 3.5 %all-to-all-start.3 = ((f32[16,1,1280]{2,1,0:T(1,128)}), f32[16,1,1280]{2,1,0:T(1,128)S(1)}, u32[]{:S(2)}, u32[]{:S(2)}) async-start(f32[16,1,1280]{2,1,0:T(1,128)} %reshape.235), calls=%async_computation.3 | async-start | bytes 163840 | tf_op jit(solution)/shard_map/all_to_all | solution.py:120
  131.9 9.2 %all-to-all-done.3 = f32[16,1,1280]{2,1,0:T(1,128)S(1)} async-done(((f32[16,1,1280]{2,1,0:T(1,128)}), f32[16,1,1280]{2,1,0:T(1,128)S(1)}, u32[]{:S(2)}, u32[]{:S(2)}) %all-to-all-start.3) | async-done | bytes 81952 | tf_op jit(solution)/shard_map/all_to_all | solution.py:120
  148.1 3.3 %copy.164 = bf16[2,32,512]{0,2,1:T(8,128)(2,1)} copy(bf16[2,32,512]{2,1,0:T(8,128)(2,1)S(1)} %fusion.3) | data formatting | bytes 131072 | tf_op jit(solution)/shard_map/reshape | solution.py:136
  152.1 13.3 %all-to-all-start.4 = ((bf16[2,32,512]{2,0,1:T(2,128)(2,1)}), bf16[2,32,512]{2,0,1:T(2,128)(2,1)S(1)}, u32[]{:S(2)}, u32[]{:S(2)}) async-start(bf16[2,32,512]{2,0,1:T(2,128)(2,1)} %copy.148), calls=%async_computation.4 | async-start | bytes 131072 | tf_op jit(solution)/shard_map/all_to_all | solution.py:129
  165.5 8.3 %gather_fusion = bf16[2048,2]{1,0:T(8,128)(2,1)S(1)} fusion(bf16[2,16384]{0,1:T(8,128)(2,1)} %bitcast.156, s32[2048]{0:T(1024)S(1)} %fusion.94), kind=kCustom, calls=%fused_computation | custom fusion | bytes 24576 | tf_op jit(solution)/shard_map/jit(_take)/gather | solution.py:137
  175.2 8.3 %all-to-all-start.6 = ((bf16[32,2,2048]{2,1,0:T(2,128)(2,1)}), bf16[32,2,2048]{2,1,0:T(2,128)(2,1)S(1)}, u32[]{:S(2)}, u32[]{:S(2)}) async-start(bf16[32,2,2048]{2,1,0:T(2,128)(2,1)} %broadcast_in_dim.34), calls=%async_computation.6 | async-start | bytes 524288 | tf_op jit(solution)/shard_map/all_to_all | solution.py:19
  184.7 10.7 %all-to-all-done.6 = bf16[32,2,2048]{2,1,0:T(2,128)(2,1)S(1)} async-done(((bf16[32,2,2048]{2,1,0:T(2,128)(2,1)}), bf16[32,2,2048]{2,1,0:T(2,128)(2,1)S(1)}, u32[]{:S(2)}, u32[]{:S(2)}) %all-to-all-start.6) | async-done | bytes 262176 | tf_op jit(solution)/shard_map/all_to_all | solution.py:19
  195.4 5.4 %all-to-all-start.5 = ((f32[64,1,512]{2,1,0:T(1,128)}), f32[64,1,512]{2,1,0:T(1,128)S(1)}, u32[]{:S(2)}, u32[]{:S(2)}) async-start(f32[64,1,512]{2,1,0:T(1,128)} %copy.149), calls=%async_computation.5 | async-start | bytes 262144 | tf_op jit(solution)/shard_map/all_to_all | solution.py:135
  203.0 6.9 %all-to-all-done.5 = f32[64,1,512]{2,1,0:T(1,128)S(1)} async-done(((f32[64,1,512]{2,1,0:T(1,128)}), f32[64,1,512]{2,1,0:T(1,128)S(1)}, u32[]{:S(2)}, u32[]{:S(2)}) %all-to-all-start.5) | async-done | bytes 131104 | tf_op jit(solution)/shard_map/all_to_all | solution.py:135
  210.7 3.5 %all-to-all-start.7 = ((f32[16,1,4160]{2,1,0:T(1,128)}), f32[16,1,4160]{2,1,0:T(1,128)S(1)}, u32[]{:S(2)}, u32[]{:S(2)}) async-start(f32[16,1,4160]{2,1,0:T(1,128)} %broadcast_in_dim.35), calls=%async_computation.7 | async-start | bytes 540672 | tf_op jit(solution)/shard_map/all_to_all | solution.py:19
  215.0 11.6 %all-to-all-done.7 = f32[16,1,4160]{2,1,0:T(1,128)S(1)} async-done(((f32[16,1,4160]{2,1,0:T(1,128)}), f32[16,1,4160]{2,1,0:T(1,128)S(1)}, u32[]{:S(2)}, u32[]{:S(2)}) %all-to-all-start.7) | async-done | bytes 266272 | tf_op jit(solution)/shard_map/all_to_all | solution.py:19
  (88 shorter events, 31.4 us)
Async XLA Ops:
  0.6 0.9 copy-start
  6.1 22.8 %all-to-all-start = ((f32[16,1,1280]{2,1,0:T(1,128)}), f32[16,1,1280]{2,1,0:T(1,128)S(1)}, u32[]{:S(2)}, u32[]{:S(2)}) async-start(f32[16,1,1280]{2,1,0:T(1,128)} %reshape.229), calls=%async_computation | async-start | bytes 163840 | tf_op jit(solution)/shard_map/all_to_all | solution.py:69
  44.8 16.8 %copy-start.1 = (f32[64,64]{1,0:T(8,128)S(1)}, f32[64,64]{1,0:T(8,128)}, u32[]{:S(2)}) copy-start(f32[64,64]{1,0:T(8,128)} %param.7) | copy-start | bytes 49156
  44.8 16.9 %copy-start.2 = (f32[32,512]{1,0:T(8,128)S(1)}, f32[32,512]{1,0:T(8,128)}, u32[]{:S(2)}) copy-start(f32[32,512]{1,0:T(8,128)} %param.6) | copy-start | bytes 196612
  58.1 16.2 %all-to-all-start.1 = ((f32[16,1,5120]{2,1,0:T(1,128)}), f32[16,1,5120]{2,1,0:T(1,128)S(1)}, u32[]{:S(2)}, u32[]{:S(2)}) async-start(f32[16,1,5120]{2,1,0:T(1,128)} %reshape.231), calls=%async_computation.1 | async-start | bytes 655360 | tf_op jit(solution)/shard_map/all_to_all | solution.py:109
  89.6 12.9 %copy-start.3 = (s32[2048]{0:T(1024)S(1)}, s32[2048]{0:T(1024)}, u32[]{:S(2)}) copy-start(s32[2048]{0:T(1024)} %param.8) | copy-start | bytes 24580
  98.8 12.7 %all-to-all-start.2 = ((f32[16,1,1280]{2,1,0:T(1,128)}), f32[16,1,1280]{2,1,0:T(1,128)S(1)}, u32[]{:S(2)}, u32[]{:S(2)}) async-start(f32[16,1,1280]{2,1,0:T(1,128)} %reshape.233), calls=%async_computation.2 | async-start | bytes 163840 | tf_op jit(solution)/shard_map/all_to_all | solution.py:69
  128.4 12.7 %all-to-all-start.3 = ((f32[16,1,1280]{2,1,0:T(1,128)}), f32[16,1,1280]{2,1,0:T(1,128)S(1)}, u32[]{:S(2)}, u32[]{:S(2)}) async-start(f32[16,1,1280]{2,1,0:T(1,128)} %reshape.235), calls=%async_computation.3 | async-start | bytes 163840 | tf_op jit(solution)/shard_map/all_to_all | solution.py:120
  148.1 53.0 %copy-start.4 = (f32[2048]{0:T(1024)S(1)}, f32[2048]{0:T(1024)}, u32[]{:S(2)}) copy-start(f32[2048]{0:T(1024)} %param.9) | copy-start | bytes 24580
  152.1 22.2 %all-to-all-start.4 = ((bf16[2,32,512]{2,0,1:T(2,128)(2,1)}), bf16[2,32,512]{2,0,1:T(2,128)(2,1)S(1)}, u32[]{:S(2)}, u32[]{:S(2)}) async-start(bf16[2,32,512]{2,0,1:T(2,128)(2,1)} %copy.148), calls=%async_computation.4 | async-start | bytes 131072 | tf_op jit(solution)/shard_map/all_to_all | solution.py:129
  175.2 20.2 %all-to-all-start.6 = ((bf16[32,2,2048]{2,1,0:T(2,128)(2,1)}), bf16[32,2,2048]{2,1,0:T(2,128)(2,1)S(1)}, u32[]{:S(2)}, u32[]{:S(2)}) async-start(bf16[32,2,2048]{2,1,0:T(2,128)(2,1)} %broadcast_in_dim.34), calls=%async_computation.6 | async-start | bytes 524288 | tf_op jit(solution)/shard_map/all_to_all | solution.py:19
  195.4 14.4 %all-to-all-start.5 = ((f32[64,1,512]{2,1,0:T(1,128)}), f32[64,1,512]{2,1,0:T(1,128)S(1)}, u32[]{:S(2)}, u32[]{:S(2)}) async-start(f32[64,1,512]{2,1,0:T(1,128)} %copy.149), calls=%async_computation.5 | async-start | bytes 262144 | tf_op jit(solution)/shard_map/all_to_all | solution.py:135
  210.7 15.8 %all-to-all-start.7 = ((f32[16,1,4160]{2,1,0:T(1,128)}), f32[16,1,4160]{2,1,0:T(1,128)S(1)}, u32[]{:S(2)}, u32[]{:S(2)}) async-start(f32[16,1,4160]{2,1,0:T(1,128)} %broadcast_in_dim.35), calls=%async_computation.7 | async-start | bytes 540672 | tf_op jit(solution)/shard_map/all_to_all | solution.py:19
where the time goes:
time: 232 us; the launch traced here: 228 us
  waiting for transfers between devices  69 us (30%)
  starting transfers between devices  54.9 us (24%)
  local copies, waits for them, and re-layouts  54.6 us (24%)
  matrix products  41.9 us (18%)
  other arithmetic  6.4 us (3%)
    unnamed x18, local copies, waits for them, and re-layouts  23.9 us
    all_to_all x2, waiting for transfers between devices, copy_for_each(): lax.all_to_all(jnp.broadcast_to(value[None], (peers, *value.shape)), axis...  22.3 us
    all_to_all x2, waiting for transfers between devices, advance_model_once(): lax.all_to_all(columns, 'space', split_axis=3, concat_axis=2, tiled=True)  21.8 us
    all_to_all x2, waiting for transfers between devices, rows_to_modes(): lax.all_to_all(stacked, 'space', split_axis=2, concat_axis=3, tiled=True)  18 us
    all_to_all x2, starting transfers between devices, rows_to_modes(): lax.all_to_all(stacked, 'space', split_axis=2, concat_axis=3, tiled=True)  17.3 us
    all_to_all x1, starting transfers between devices, on_device(): lax.all_to_all(rounded, 'member', split_axis=1, concat_axis=0, tiled=True)  13.3 us
    all_to_all x2, starting transfers between devices, copy_for_each(): lax.all_to_all(jnp.broadcast_to(value[None], (peers, *value.shape)), axis...  11.8 us
    gather x1, local copies, waits for them, and re-layouts, on_device(): picked = jnp.take(flat, probes, axis=1)  8.33 us
  transfers between devices with their start and end apart: 8, of which 7 were waited for; matrix products, arithmetic and copies ran while one was open for 6% of the time, Pallas kernels for 0%

commit v1 on v0

v1 whole, which is shorter than its diff:
```python
import math

import jax
import jax.numpy as jnp
import ml_dtypes
import numpy as np
from jax import lax
from jax.experimental import pallas as pl
from jax.experimental.pallas import tpu as pltpu
from jax.sharding import PartitionSpec as P

N = 512
KEEP = 160
DT_STEP = 0.1
VISCOSITY = 0.05
MEMBERS = 64
ROWS = 32
PROBES = 32768
GM = 32
GS = 16
W = KEEP // GS
QP = 384
SWAP = False

F32 = jnp.float32
BF16 = jnp.bfloat16
MESH = pl.DeviceIdType.MESH
NN = (((1,), (0,)), ((), ()))
NT = (((1,), (1,)), ((), ()))


def halves(table):
    high = table.astype(np.float32).astype(ml_dtypes.bfloat16)
    low = (table - high.astype(np.float64)).astype(np.float32).astype(ml_dtypes.bfloat16)
    return [high, low]


def make_tables():
    cells = np.arange(N)
    slots = np.arange(2 * KEEP)
    kx = np.where(slots < KEEP, slots, slots - 2 * KEEP)
    ky = np.arange(KEEP)

    def trig(a, b):
        angle = (a[:, None] * b[None, :] % N) * (2.0 * np.pi / N)
        return np.cos(angle), np.sin(angle)

    cos_y, sin_y = trig(ky, cells)
    rows_f = np.concatenate([cos_y, -sin_y], 1)
    cos_x, sin_x = trig(cells, kx)
    cols_f = np.zeros((2 * N, QP))
    cols_f[:N, : 2 * KEEP] = cos_x / (N * N)
    cols_f[N:, : 2 * KEEP] = sin_x / (N * N)
    cols_g = np.zeros((2 * QP, N))
    cols_g[: 2 * KEEP] = cos_x.T
    cols_g[QP : QP + 2 * KEEP] = sin_x.T
    count = np.where(ky == 0, 1.0, 2.0)[:, None]
    rows_g4 = np.stack([cos_y * count, -sin_y * count], 0)
    rows_g4 = rows_g4.reshape(2, GS, W, N).transpose(1, 0, 2, 3).reshape(2 * KEEP, N).T
    out = []
    for t in (rows_f, cols_f, cols_g, rows_g4, cos_y * count, -sin_y * count):
        out += halves(np.ascontiguousarray(t))
    return out


TABLE_SHAPES = [(KEEP, 2 * N), (2 * N, QP), (2 * QP, N), (N, 2 * KEEP), (KEEP, N), (KEEP, N)]


def dot(a, b, dims=NN):
    return lax.dot_general(a, b, dims, preferred_element_type=F32)


def split(x):
    high = x.astype(BF16)
    return high, (x - high.astype(F32)).astype(BF16)


def swap(m, s):
    if not SWAP:
        return m, s
    z_lo, y, core = lax.div(m, 16), lax.rem(lax.div(m, 2), 8), lax.rem(m, 2)
    x, z_hi = lax.div(s, 4), lax.rem(s, 4)
    return lax.div(z_hi, 2) * 16 + y * 2 + lax.rem(z_hi, 2), x * 4 + z_lo * 2 + core


def lane_group(shape):
    return lax.div(lax.broadcasted_iota(jnp.int32, shape, len(shape) - 1), 32)


def pick_groups(pieces):
    group = lane_group(pieces[0].shape)
    low = jnp.where(group == 0, pieces[0], pieces[1])
    high = jnp.where(group == 2, pieces[2], pieces[3])
    return jnp.where(group < 2, low, high)


def turn(x, groups):
    groups %= 4
    return x if groups == 0 else pltpu.roll(x, 32 * groups, 1)


def gather_columns(recv):
    by_slot = [
        jnp.concatenate([recv[pl.ds(W * (4 * hi + slot), 16), :] for hi in range(4)], 0)
        for slot in range(4)
    ]
    rows = []
    for m in range(2):
        for c in range(2):
            t = c * 2 + m
            got = pick_groups([turn(by_slot[slot], slot - t) for slot in range(4)])
            rows.append(jnp.concatenate([got[16 * hi : 16 * hi + 16] for hi in range(4)], 1))
    return jnp.concatenate(rows, 0)


def times_i(w):
    return jnp.concatenate([-w[16:32], w[0:16], -w[48:64], w[32:48]], 0)


def to_slots(d, t_high, t_low):
    both = jnp.concatenate([d, -times_i(d)], 1)
    high, low = split(both)
    out = dot(jnp.concatenate([high, low], 0), t_high)
    return out[:64] + out[64:] + dot(high, t_low)


def to_cells(lhs, t_high, t_low):
    rows = lhs.shape[0]
    high, low = split(lhs)
    out = dot(jnp.concatenate([high, low], 0), t_high)
    return out[:rows] + out[rows:] + dot(high, t_low)


def stack_lanes(x):
    return jnp.concatenate([x[:, 128 * i : 128 * i + 128] for i in range(4)], 0)


def kernel(
    swirls, driving, mixing, probes, observed, *rest
):
    tables_hbm = rest[:12]
    analysis, spread, projection = rest[12:15]
    (
        f_v, drive_in, drive, mix_v, probes_v, obs_v,
        *more
    ) = rest[15:]
    tables = more[:12]
    (
        send1, recv1, send2, recv2, send3, recv3, send4, recv4, send5, recv5, send6, recv6,
        hist_s, hist_r, send_a, recv_a, send_b, recv_b, send_c, recv_c,
        spectrum, members_v, mixed_v,
        load_sem, table_sem, send_sem, recv_sem,
    ) = more[12:]
    m, s = lax.axis_index("member"), lax.axis_index("space")
    vm, vs = swap(m, s)

    def there(target):
        return dict(device_id={"member": target[0], "space": target[1]}, device_id_type=MESH)

    barrier = pltpu.get_barrier_semaphore()

    def hello(target):
        pl.semaphore_signal(barrier, inc=1, **there(target))

    greeted = (GS - 1) + (GM - 1)

    @pl.loop(1, GS)
    def _(d):
        hello(swap(vm, lax.rem(vs + d, GS)))

    @pl.loop(1, GM)
    def _(d):
        hello(swap(lax.rem(vm + d, GM), vs))

    if SWAP:
        @pl.loop(0, GS)
        def _(p):
            @pl.when(jnp.logical_or(vm != m, p != s))
            def _():
                hello((vm, p))

        @pl.loop(0, GM)
        def _(a):
            @pl.when(jnp.logical_or(vs != s, a != vm))
            def _():
                hello(swap(a, s))

        greeted = greeted + GS + GM - (vm == m).astype(jnp.int32) - (vs == s).astype(jnp.int32)

    loads = [
        pltpu.make_async_copy(src, dst, load_sem.at[i])
        for i, (src, dst) in enumerate(
            [(swirls, f_v), (driving, drive_in), (mixing, mix_v), (probes, probes_v), (observed, obs_v)]
        )
    ]
    table_loads = [
        pltpu.make_async_copy(src, dst, table_sem.at[i])
        for i, (src, dst) in enumerate(zip(tables_hbm, tables))
    ]
    loads[0].start()
    for copy in table_loads[:2]:
        copy.start()
    for copy in loads[1:]:
        copy.start()
    for copy in table_loads[2:]:
        copy.start()

    pending = []

    def copy_out(k, src, dst, target):
        return pltpu.make_async_remote_copy(
            src_ref=src, dst_ref=dst, send_sem=send_sem.at[k], recv_sem=recv_sem.at[k], **there(target)
        )

    def exchange(k, src, dst, axis, many=True):
        n = GS if axis == "space" else GM
        me = vs if axis == "space" else vm
        pltpu.make_async_copy(src(me), dst(me), recv_sem.at[k]).start()

        @pl.loop(1, n)
        def _(d):
            p = lax.rem(me + d, n)
            copy_out(k, src(p), dst(me), swap(vm, p) if axis == "space" else swap(p, vs)).start()

    def scatter(k, n, src, dst, target, is_self):
        @pl.loop(0, n)
        def _(p):
            mine = is_self(p)

            @pl.when(mine)
            def _():
                pltpu.make_async_copy(src(p), dst, recv_sem.at[k]).start()

            @pl.when(jnp.logical_not(mine))
            def _():
                copy_out(k, src(p), dst, target(p)).start()

    def finish(k, ref):
        pltpu.make_async_copy(ref, ref, recv_sem.at[k]).wait()

    def rows_of(ref, count):
        return lambda p: ref.at[pl.ds(count * p, count)]

    loads[0].wait()
    high, low = split(f_v[...])
    zero = jnp.zeros_like(high)

    def apart(x):
        return jnp.concatenate(
            [jnp.concatenate([x, zero], 1), jnp.concatenate([zero, x], 1)], 0
        )

    rhs_high = apart(high)
    table_loads[0].wait()
    table_loads[1].wait()
    out = dot(tables[0][...], jnp.concatenate([rhs_high, apart(low)], 0), NT)
    send1[...] = out[:, :128] + out[:, 128:] + dot(tables[1][...], rhs_high, NT)

    pl.semaphore_wait(barrier, greeted)
    if SWAP:
        scatter(
            0, GS, rows_of(send1, W), recv1.at[pl.ds(W * s, W)], lambda p: swap(m, p),
            lambda p: jnp.logical_and(vm == m, p == vs),
        )
    else:
        exchange(0, rows_of(send1, W), rows_of(recv1, W), "space")

    for copy in loads[1:]:
        copy.wait()
    if SWAP:
        @pl.when(jnp.logical_and(vm == m, vs == s))
        def _():
            pltpu.make_async_copy(drive_in, drive, recv_sem.at[10]).start()

        @pl.when(jnp.logical_or(vm != m, vs != s))
        def _():
            copy_out(10, drive_in, drive, (vm, vs)).start()
    tail = pl.ds(KEEP, 8)
    recv1[tail, :] = jnp.zeros((8, 128), F32)
    recv3[tail, :] = jnp.zeros((8, 128), F32)
    columns = lax.broadcasted_iota(jnp.int32, (N, 128), 0) + m * N

    def tally(i, total):
        cell = probes_v[pl.ds(i, 1), :]
        obs = obs_v[pl.ds(i, 1), :]
        a, rest_ = split(obs)
        left = obs - a.astype(F32)
        b = left.astype(BF16)
        c = (left - b.astype(F32)).astype(BF16)
        ones = jnp.ones((1, 128), BF16)
        lhs = jnp.concatenate([ones, a, b, c], 0)
        hit = jnp.where(columns == cell, 1.0, 0.0).astype(BF16)
        return total + dot(lhs, hit, NT)

    total = lax.fori_loop(0, 16, tally, jnp.zeros((4, N), F32))
    sums = total[1:2] + total[2:3] + total[3:4]
    for i in range(4):
        hist_s[i : i + 1, :] = total[0:1, 128 * i : 128 * i + 128]
        hist_s[4 + i : 5 + i, :] = sums[:, 128 * i : 128 * i + 128]
    if SWAP:
        @pl.when(jnp.logical_and(vm == m, vs == s))
        def _():
            pltpu.make_async_copy(hist_s, hist_r, recv_sem.at[11]).start()

        @pl.when(jnp.logical_or(vm != m, vs != s))
        def _():
            copy_out(11, hist_s, hist_r, (vm, vs)).start()
    weights = mix_v[...]
    weights = weights + (1.0 - jnp.sum(weights, 0, keepdims=True)) * (1.0 / MEMBERS)
    weights = weights.T
    w_high, w_rest = split(weights)
    w_left = weights - w_high.astype(F32)
    w_mid = w_left.astype(BF16)
    w_low = (w_left - w_mid.astype(F32)).astype(BF16)
    w_parts = jnp.concatenate([w_high, w_mid, w_low], 0)
    for copy in table_loads[2:]:
        copy.wait()

    scale = 2.0 * math.pi / N
    slot = lax.broadcasted_iota(jnp.int32, (16, QP), 1)
    slot = jnp.where(slot < KEEP, slot, jnp.where(slot < 2 * KEEP, slot - 2 * KEEP, 0))
    wave_x = slot.astype(F32) * scale
    wave_y = (lax.broadcasted_iota(jnp.int32, (16, QP), 0) + vs * W).astype(F32) * scale
    squared = wave_x * wave_x + wave_y * wave_y
    inverse = jnp.where(squared > 0, 1.0 / jnp.where(squared > 0, squared, 1.0), 0.0)

    def for_all(x):
        return jnp.concatenate([x] * 4, 0)

    finish(0, recv1.at[pl.ds(0, KEEP)])
    w = to_slots(gather_columns(recv1), tables[2][...], tables[3][...])
    spectrum[...] = w
    iw = times_i(w)
    pairs = [(wave_y * inverse, -wave_x * inverse), (wave_x, wave_y)]
    for h, pair in enumerate(pairs):
        lhs = jnp.concatenate(
            [jnp.concatenate([for_all(u) * iw, for_all(u) * -w], 1) for u in pair], 0
        )
        e = to_cells(lhs, tables[4][...], tables[5][...])
        parts = [stack_lanes(e[32 * g : 32 * g + 32]) for g in range(4)]
        for slot_ in range(4):
            got = pick_groups([turn(parts[g], g - slot_) for g in range(4)])
            for hi in range(4):
                for c in range(2):
                    send2[h, pl.ds(2 * W * (4 * hi + slot_) + W * c, W), :] = got[
                        32 * hi + 16 * c : 32 * hi + 16 * c + W
                    ]
        exchange(1 + h, rows_of(send2.at[h], 2 * W), rows_of(recv2.at[h], 2 * W), "space")

    def to_rows(h):
        high, low = split(recv2[h])
        out = dot(tables[6][...], jnp.concatenate([high, low], 1))
        return out[:, :128] + out[:, 128:] + dot(tables[7][...], high)

    finish(1, recv2.at[0])
    velocity = to_rows(0)
    finish(2, recv2.at[1])
    product = velocity * to_rows(1)
    product = product + pltpu.roll(product, 64, 1)
    first = lax.broadcasted_iota(jnp.int32, product.shape, 1) < 64
    rhs = jnp.concatenate([jnp.where(first, product, 0.0), jnp.where(first, 0.0, product)], 0)
    high, low = split(rhs)
    out = dot(tables[0][...], jnp.concatenate([high, low], 1))
    send3[...] = out[:, :128] + out[:, 128:] + dot(tables[1][...], high)
    exchange(3, rows_of(send3, W), rows_of(recv3, W), "space")

    finish(3, recv3.at[pl.ds(0, KEEP)])
    adv = to_slots(gather_columns(recv3), tables[2][...], tables[3][...])
    w = spectrum[...]
    new = w + DT_STEP * (-adv - VISCOSITY * for_all(squared) * w)
    e = to_cells(jnp.concatenate([new, times_i(new)], 1), tables[4][...], tables[5][...])
    parts = {
        c * 2 + k: stack_lanes(e[32 * k + 16 * c : 32 * k + 16 * c + 16])
        for k in range(2) for c in range(2)
    }
    for slot_ in range(4):
        got = pick_groups([turn(parts[g], g - slot_) for g in range(4)])
        for hi in range(4):
            send4[pl.ds(W * (4 * hi + slot_), W), :] = got[16 * hi : 16 * hi + W]
    exchange(4, rows_of(send4, W), rows_of(recv4, W), "space")

    if SWAP:
        finish(10, drive)
        finish(11, hist_r)
        drive_ref, hist = drive, hist_r
    else:
        drive_ref, hist = drive_in, hist_s
    forcing = DT_STEP * drive_ref[...]
    counts = jnp.concatenate([hist[i : i + 1, :] for i in range(4)], 1)
    obs_sums = jnp.concatenate([hist[4 + i : 5 + i, :] for i in range(4)], 1)

    finish(4, recv4)
    modes = recv4[...].T
    high, low = split(modes)
    out = dot(jnp.concatenate([high[:64], low[:64]], 0), tables[8][...])
    out = out + dot(jnp.concatenate([high[64:], low[64:]], 0), tables[10][...])
    fresh = out[:64] + out[64:] + dot(high[:64], tables[9][...]) + dot(high[64:], tables[11][...])
    fresh = fresh + jnp.concatenate([forcing, forcing], 0)
    rounded = fresh.astype(BF16).astype(F32)
    for k in range(2):
        for i in range(4):
            send5[:, 4 * k + i, :] = rounded[32 * k : 32 * k + 32, 128 * i : 128 * i + 128]
    exchange(5, lambda p: send5.at[p], lambda p: recv5.at[p], "member")

    finish(5, recv5)
    for k in range(2):
        for i in range(4):
            members_v[i, pl.ds(k, 32, stride=2), :] = recv5[:, 4 * k + i, :]
    values = jnp.concatenate([members_v[i] for i in range(4)], 1)

    centre = jnp.sum(values, 0, keepdims=True) * (1.0 / MEMBERS)
    anomaly = values - centre
    innovation = obs_sums - counts * centre
    other = jnp.concatenate(
        [anomaly * counts, innovation, jnp.zeros((63, N), F32)], 0
    )
    a_high, a_low = split(anomaly)
    b_high, b_low = split(other)
    send_a[...] = dot(a_high, b_high, NT) + dot(a_high, b_low, NT) + dot(a_low, b_high, NT)
    exchange(7, rows_of(send_a, 4), rows_of(recv_a, 4), "space")

    mixed = dot(w_parts, values.astype(BF16))
    mixed = mixed[:64] + mixed[64:128] + mixed[128:]
    for i in range(4):
        mixed_v[i] = mixed[:, 128 * i : 128 * i + 128]
    for k in range(2):
        for i in range(4):
            send6[:, 4 * k + i, :] = mixed_v[i, pl.ds(k, 32, stride=2), :]
    if SWAP:
        scatter(
            6, GM, lambda p: send6.at[p], recv6.at[vm], lambda p: (p, vs),
            lambda p: jnp.logical_and(vs == s, p == m),
        )
    else:
        exchange(6, lambda p: send6.at[p], lambda p: recv6.at[p], "member")

    finish(7, recv_a)
    chunk = recv_a[pl.ds(0, 4), :]
    for p in range(1, GS):
        chunk = chunk + recv_a[pl.ds(4 * p, 4), :]
    send_b[...] = chunk
    exchange(8, lambda p: send_b, rows_of(recv_b, 4), "member")

    finish(6, recv6)
    for k in range(2):
        for i in range(4):
            analysis[k, :, pl.ds(128 * i, 128)] = recv6[:, 4 * k + i, :]

    finish(8, recv_b)
    chunk = recv_b[pl.ds(0, 4), :]
    for p in range(1, GM):
        chunk = chunk + recv_b[pl.ds(4 * p, 4), :]
    send_c[...] = chunk
    exchange(9, lambda p: send_c, rows_of(recv_c, 4), "space")
    finish(9, recv_c)
    full = recv_c[...]
    spread[...] = full[:, :64] * (1.0 / PROBES)
    shape = (64, 64)
    diagonal = lax.broadcasted_iota(jnp.int32, shape, 0) == lax.broadcasted_iota(jnp.int32, shape, 1)
    column = jnp.where(diagonal, full[:, 64:65], 0.0)
    projection[...] = jnp.sum(column, 0, keepdims=True) * (1.0 / math.sqrt(PROBES))

    others = {
        0: send1.at[pl.ds(0, W * (GS - 1))],
        1: send2.at[0, pl.ds(0, 2 * W * (GS - 1))],
        2: send2.at[1, pl.ds(0, 2 * W * (GS - 1))],
        3: send3.at[pl.ds(0, W * (GS - 1))],
        4: send4.at[pl.ds(0, W * (GS - 1))],
        5: send5.at[pl.ds(0, GM - 1)],
        6: send6.at[pl.ds(0, GM - 1)],
        7: send_a.at[pl.ds(0, 4 * (GS - 1))],
        8: recv_b.at[pl.ds(0, 4 * (GM - 1))],
        9: recv_c.at[pl.ds(0, 4 * (GS - 1))],
    }

    def sent(k, ref):
        pltpu.make_async_copy(ref, ref, send_sem.at[k]).wait()

    for k, ref in others.items():
        sent(k, ref)
    if SWAP:
        @pl.when(vm != m)
        def _():
            sent(0, send1.at[pl.ds(0, W)])

        @pl.when(vs != s)
        def _():
            sent(6, send6.at[0])

        @pl.when(jnp.logical_or(vm != m, vs != s))
        def _():
            sent(10, drive_in)
            sent(11, hist_s)


def on_device(swirls, driving, mixing, probes, observed):
    tables = [jnp.asarray(t) for t in make_tables()]
    vmem = pltpu.VMEM
    lanes = 128
    buffers = [
        (64, N), (ROWS, N), (ROWS, N), (64, 64),
    ]
    scratch = [vmem(shape, F32) for shape in buffers]
    scratch += [vmem((16, 128), jnp.int32), vmem((16, 128), F32)]
    for shape in TABLE_SHAPES:
        scratch += [vmem(shape, BF16)] * 2
    for shape in [
        (KEEP, lanes), (KEEP + 8, lanes),
        (2, 2 * KEEP, lanes), (2, 2 * KEEP, lanes),
        (KEEP, lanes), (KEEP + 8, lanes),
        (KEEP, lanes), (KEEP, lanes),
        (GM, 8, lanes), (GM, 8, lanes), (GM, 8, lanes), (GM, 8, lanes),
        (8, lanes), (8, lanes),
        (64, lanes), (64, lanes), (4, lanes), (4 * GM, lanes), (4, lanes), (64, lanes),
        (64, QP), (4, 64, lanes), (4, 64, lanes),
    ]:
        scratch.append(vmem(shape, F32))
    dma = pltpu.SemaphoreType.DMA
    scratch += [dma((5,)), dma((12,)), dma((12,)), dma((12,))]
    anywhere = pl.BlockSpec(memory_space=pl.ANY)
    analysis, spread, projection = pl.pallas_call(
        kernel,
        out_shape=[
            jax.ShapeDtypeStruct((2, ROWS, N), F32),
            jax.ShapeDtypeStruct((64, 64), F32),
            jax.ShapeDtypeStruct((1, 64), F32),
        ],
        in_specs=[anywhere] * (5 + len(tables)),
        out_specs=[pl.BlockSpec(memory_space=pltpu.VMEM)] * 3,
        scratch_shapes=scratch,
        compiler_params=pltpu.CompilerParams(
            collective_id=0, has_side_effects=True, vmem_limit_bytes=48 * 2**20
        ),
    )(
        swirls.reshape(64, N), driving, mixing, probes.reshape(16, 128), observed.reshape(16, 128),
        *tables,
    )
    return analysis, spread, projection.reshape(64)


def solution(mesh):
    return jax.shard_map(
        on_device,
        mesh=mesh,
        in_specs=(P("member", "space", None), P("space", None), P(), P("space"), P("space")),
        out_specs=(P("member", "space", None), P(), P()),
        check_vma=False,
    )
```

time: 232 us -> 91.1 us (0.39); the launches traced: 228 us -> 90.3 us
  Pallas kernels: 0 us -> 71.9 us
  waiting for transfers between devices: 69 us -> 0 us
  starting transfers between devices: 54.9 us -> 0 us
  matrix products: 41.9 us -> 0 us
  local copies, waits for them, and re-layouts: 54.6 us -> 17.8 us
  other arithmetic: 6.4 us -> 0 us
    pallas_call x0 -> x1, Pallas kernels: none -> 71.9 us  [on_device(): pl.pallas_call(kernel, out_shape=[jax.ShapeDtypeStruct((2, ROWS, N), F32)...]
    all_to_all x8 -> x0, waiting for transfers between devices: 69 us -> none  [the longest x2 22.3 us: copy_for_each(): lax.all_to_all(jnp.broadcast_to(value[None], (peers, *value.shape)), axis...]
    all_to_all x8 -> x0, starting transfers between devices: 54.9 us -> none  [the longest x2 17.3 us: rows_to_modes(): lax.all_to_all(stacked, 'space', split_axis=2, concat_axis=3, tiled=True)]
    dot_general x19 -> x0, matrix products: 41.9 us -> none  [the longest x2 7.13 us: modes_to_columns(): jnp.einsum('bpkq,nq->bpkn', stacked, precomputed_trig[3], precision=EXACT)]
    all_to_all x9 -> x0, local copies, waits for them, and re-layouts: 8.5 us -> none  [the longest x3 6.85 us: advance_model_once(): lax.all_to_all(columns, 'space', split_axis=3, concat_axis=2, tiled=True)]
    gather x1 -> x0, local copies, waits for them, and re-layouts: 8.33 us -> none  [on_device(): picked = jnp.take(flat, probes, axis=1)]
    unnamed x18 -> x37, local copies, waits for them, and re-layouts: 23.9 us -> 17.8 us
    another operation x4 -> x0, local copies, waits for them, and re-layouts: 5.66 us -> none  [the longest x2 5.21 us: modes_to_columns(): jnp.stack([with_cos[:, 0] - with_sin[:, 1], with_sin[:, 0] + with_cos[:,...]
  transfers between devices with their start and end apart: 8 -> 0, of which waited for: 7 -> 0; matrix products, arithmetic and copies ran while one was open for 6% -> 0% of each run, Pallas kernels for 0% -> 0%
where the time goes in v1:
time: 91.1 us; the launch traced here: 90.3 us
  Pallas kernels  71.9 us (79%)
  local copies, waits for them, and re-layouts  17.8 us (20%)
    pallas_call x1, Pallas kernels, on_device(): pl.pallas_call(kernel, out_shape=[jax.ShapeDtypeStruct((2, ROWS, N), F32)...  71.9 us
    unnamed x37, local copies, waits for them, and re-layouts  17.8 us

profile of v1, /device:TPU:1, one launch (start us, length us, event | category | flops | bytes accessed | tf_op | source)
XLA Modules:
  0.0 90.3 jit_solution(14825250317774732584)
XLA Ops:
  0.6 0.0 copy-start
  0.6 1.1 %copy-done = bf16[768,512]{1,0:T(8,128)(2,1)S(1)} copy-done((bf16[768,512]{1,0:T(8,128)(2,1)S(1)}, bf16[768,512]{1,0:T(8,128)(2,1)}, u32[]{:S(2)}) %copy-start) | copy-done | bytes 786456
  1.8 0.0 copy-start.1
  1.8 1.1 %copy-done.1 = bf16[768,512]{1,0:T(8,128)(2,1)S(1)} copy-done((bf16[768,512]{1,0:T(8,128)(2,1)S(1)}, bf16[768,512]{1,0:T(8,128)(2,1)}, u32[]{:S(2)}) %copy-start.1) | copy-done | bytes 786456
  2.9 0.0 copy-start.2
  2.9 1.1 %copy-done.2 = bf16[1024,384]{1,0:T(8,128)(2,1)S(1)} copy-done((bf16[1024,384]{1,0:T(8,128)(2,1)S(1)}, bf16[1024,384]{1,0:T(8,128)(2,1)}, u32[]{:S(2)}) %copy-start.2) | copy-done | bytes 786456
  4.0 0.0 copy-start.3
  4.0 1.1 %copy-done.3 = bf16[1024,384]{1,0:T(8,128)(2,1)S(1)} copy-done((bf16[1024,384]{1,0:T(8,128)(2,1)S(1)}, bf16[1024,384]{1,0:T(8,128)(2,1)}, u32[]{:S(2)}) %copy-start.3) | copy-done | bytes 786456
  5.2 0.0 copy-start.4
  5.2 1.0 %copy-done.4 = bf16[512,320]{1,0:T(8,128)(2,1)S(1)} copy-done((bf16[512,320]{1,0:T(8,128)(2,1)S(1)}, bf16[512,320]{1,0:T(8,128)(2,1)}, u32[]{:S(2)}) %copy-start.4) | copy-done | bytes 327704
  6.2 0.0 copy-start.5
  6.2 1.0 %copy-done.5 = bf16[512,320]{1,0:T(8,128)(2,1)S(1)} copy-done((bf16[512,320]{1,0:T(8,128)(2,1)S(1)}, bf16[512,320]{1,0:T(8,128)(2,1)}, u32[]{:S(2)}) %copy-start.5) | copy-done | bytes 327704
  7.2 0.0 copy-start.6
  7.2 1.0 %copy-done.6 = bf16[160,1024]{1,0:T(8,128)(2,1)S(1)} copy-done((bf16[160,1024]{1,0:T(8,128)(2,1)S(1)}, bf16[160,1024]{1,0:T(8,128)(2,1)}, u32[]{:S(2)}) %copy-start.6) | copy-done | bytes 327704
  8.1 0.0 copy-start.7
  8.1 1.0 %copy-done.7 = bf16[160,1024]{1,0:T(8,128)(2,1)S(1)} copy-done((bf16[160,1024]{1,0:T(8,128)(2,1)S(1)}, bf16[160,1024]{1,0:T(8,128)(2,1)}, u32[]{:S(2)}) %copy-start.7) | copy-done | bytes 327704
  9.1 0.0 copy-start.8
  9.1 0.9 %copy-done.8 = bf16[160,512]{1,0:T(8,128)(2,1)S(1)} copy-done((bf16[160,512]{1,0:T(8,128)(2,1)S(1)}, bf16[160,512]{1,0:T(8,128)(2,1)}, u32[]{:S(2)}) %copy-start.8) | copy-done | bytes 163864
  10.0 0.0 copy-start.9
  10.0 0.9 %copy-done.9 = bf16[160,512]{1,0:T(8,128)(2,1)S(1)} copy-done((bf16[160,512]{1,0:T(8,128)(2,1)S(1)}, bf16[160,512]{1,0:T(8,128)(2,1)}, u32[]{:S(2)}) %copy-start.9) | copy-done | bytes 163864
  10.9 0.0 copy-start.10
  10.9 0.9 %copy-done.10 = bf16[160,512]{1,0:T(8,128)(2,1)S(1)} copy-done((bf16[160,512]{1,0:T(8,128)(2,1)S(1)}, bf16[160,512]{1,0:T(8,128)(2,1)}, u32[]{:S(2)}) %copy-start.10) | copy-done | bytes 163864
  11.9 0.9 %copy-done.11 = bf16[160,512]{1,0:T(8,128)(2,1)S(1)} copy-done((bf16[160,512]{1,0:T(8,128)(2,1)S(1)}, bf16[160,512]{1,0:T(8,128)(2,1)}, u32[]{:S(2)}) %copy-start.11) | copy-done | bytes 163864
  12.8 0.9 copy-done.12
  13.7 0.8 copy-done.13
  14.5 0.8 copy-done.14
  15.3 0.7 copy-done.15
  16.0 0.7 copy-done.16
  16.7 71.9 %shard_map.184 = (f32[2,32,512]{2,1,0:T(8,128)S(1)}, f32[64,64]{1,0:T(8,128)S(1)}, f32[1,64]{1,0:T(1,128)S(1)}) custom-call(f32[64,512]{1,0:T(8,128)S(1)} %bitcast.4, f32[32,512]{1,0:T(8,128)S(1)} %copy-done.13, f32[64,64]{1,0:T(8,128)S(1)} %copy-done.14, s32[16,128]{1,0:T(8,128)S(1)} %bitcast.5, f32[16,128]{1,0:T(8,128)S(1)} %bitcast.6, ...), custom_call_target="tpu_custom_call" | custom-call | tf_op jit(solution)/shard_map/pallas_call | solution.py:521
  88.6 0.7 copy.23
  89.2 0.6 copy.24
  89.8 0.5 copy.25
  (6 shorter events, 0.0 us)
Async XLA Ops:
  0.6 1.1 %copy-start = (bf16[768,512]{1,0:T(8,128)(2,1)S(1)}, bf16[768,512]{1,0:T(8,128)(2,1)}, u32[]{:S(2)}) copy-start(bf16[768,512]{1,0:T(8,128)(2,1)} %constant.29.clone.rest_5_) | copy-start | bytes 2359300
  1.8 1.1 %copy-start.1 = (bf16[768,512]{1,0:T(8,128)(2,1)S(1)}, bf16[768,512]{1,0:T(8,128)(2,1)}, u32[]{:S(2)}) copy-start(bf16[768,512]{1,0:T(8,128)(2,1)} %constant.28.clone.rest_4_) | copy-start | bytes 2359300
  2.9 1.1 %copy-start.2 = (bf16[1024,384]{1,0:T(8,128)(2,1)S(1)}, bf16[1024,384]{1,0:T(8,128)(2,1)}, u32[]{:S(2)}) copy-start(bf16[1024,384]{1,0:T(8,128)(2,1)} %constant.27.clone.rest_3_) | copy-start | bytes 2359300
  4.0 1.1 %copy-start.3 = (bf16[1024,384]{1,0:T(8,128)(2,1)S(1)}, bf16[1024,384]{1,0:T(8,128)(2,1)}, u32[]{:S(2)}) copy-start(bf16[1024,384]{1,0:T(8,128)(2,1)} %constant.26.clone.rest_2_) | copy-start | bytes 2359300
  5.2 1.0 %copy-start.4 = (bf16[512,320]{1,0:T(8,128)(2,1)S(1)}, bf16[512,320]{1,0:T(8,128)(2,1)}, u32[]{:S(2)}) copy-start(bf16[512,320]{1,0:T(8,128)(2,1)} %constant.31.clone.rest_7_) | copy-start | bytes 983044
  6.2 1.0 %copy-start.5 = (bf16[512,320]{1,0:T(8,128)(2,1)S(1)}, bf16[512,320]{1,0:T(8,128)(2,1)}, u32[]{:S(2)}) copy-start(bf16[512,320]{1,0:T(8,128)(2,1)} %constant.30.clone.rest_6_) | copy-start | bytes 983044
  7.2 1.0 %copy-start.6 = (bf16[160,1024]{1,0:T(8,128)(2,1)S(1)}, bf16[160,1024]{1,0:T(8,128)(2,1)}, u32[]{:S(2)}) copy-start(bf16[160,1024]{1,0:T(8,128)(2,1)} %constant.25.clone.rest_1_) | copy-start | bytes 983044
  8.1 1.0 %copy-start.7 = (bf16[160,1024]{1,0:T(8,128)(2,1)S(1)}, bf16[160,1024]{1,0:T(8,128)(2,1)}, u32[]{:S(2)}) copy-start(bf16[160,1024]{1,0:T(8,128)(2,1)} %constant.24.clone.rest_0_) | copy-start | bytes 983044
  9.1 0.9 %copy-start.8 = (bf16[160,512]{1,0:T(8,128)(2,1)S(1)}, bf16[160,512]{1,0:T(8,128)(2,1)}, u32[]{:S(2)}) copy-start(bf16[160,512]{1,0:T(8,128)(2,1)} %constant.35.clone.rest_11_) | copy-start | bytes 491524
  10.0 0.9 %copy-start.9 = (bf16[160,512]{1,0:T(8,128)(2,1)S(1)}, bf16[160,512]{1,0:T(8,128)(2,1)}, u32[]{:S(2)}) copy-start(bf16[160,512]{1,0:T(8,128)(2,1)} %constant.34.clone.rest_10_) | copy-start | bytes 491524
  10.9 0.9 %copy-start.10 = (bf16[160,512]{1,0:T(8,128)(2,1)S(1)}, bf16[160,512]{1,0:T(8,128)(2,1)}, u32[]{:S(2)}) copy-start(bf16[160,512]{1,0:T(8,128)(2,1)} %constant.33.clone.rest_9_) | copy-start | bytes 491524
  11.9 0.9 %copy-start.11 = (bf16[160,512]{1,0:T(8,128)(2,1)S(1)}, bf16[160,512]{1,0:T(8,128)(2,1)}, u32[]{:S(2)}) copy-start(bf16[160,512]{1,0:T(8,128)(2,1)} %constant.32.clone.rest_8_) | copy-start | bytes 491524
  12.8 0.9 %copy-start.12 = (f32[2,32,512]{2,1,0:T(8,128)S(1)}, f32[2,32,512]{2,1,0:T(8,128)}, u32[]{:S(2)}) copy-start(f32[2,32,512]{2,1,0:T(8,128)} %param.17) | copy-start | bytes 393220
  13.7 0.8 copy-start.13
  14.5 0.8 copy-start.14
  15.3 0.7 copy-start.15
  16.0 0.7 copy-start.16

commit v2 on v1

--- a/solution.py
+++ b/solution.py
@@ -20,7 +20,7 @@
 GS = 16
 W = KEEP // GS
 QP = 384
-SWAP = False
+SWAP = True
 
 F32 = jnp.float32
 BF16 = jnp.bfloat16
@@ -529,7 +529,7 @@
         out_specs=[pl.BlockSpec(memory_space=pltpu.VMEM)] * 3,
         scratch_shapes=scratch,
         compiler_params=pltpu.CompilerParams(
-            collective_id=0, has_side_effects=True, vmem_limit_bytes=48 * 2**20
+            collective_id=0, has_side_effects=True, vmem_limit_bytes=60 * 2**20
         ),
     )(
         swirls.reshape(64, N), driving, mixing, probes.reshape(16, 128), observed.reshape(16, 128),

time: 91.1 us -> 73.2 us (0.80)
  local copies, waits for them, and re-layouts: 17.8 us -> 2.71 us
  Pallas kernels: 71.9 us -> 69.7 us
    unnamed x37 -> x7, local copies, waits for them, and re-layouts: 17.8 us -> 2.71 us
    pallas_call x1, Pallas kernels: 71.9 us -> 69.7 us  [on_device(): pl.pallas_call(kernel, out_shape=[jax.ShapeDtypeStruct((2, ROWS, N), F32)...]
where the time goes in v2:
time: 73.2 us; the launch traced here: 73.1 us
  Pallas kernels  69.7 us (95%)
  local copies, waits for them, and re-layouts  2.71 us (4%)
    pallas_call x1, Pallas kernels, on_device(): pl.pallas_call(kernel, out_shape=[jax.ShapeDtypeStruct((2, ROWS, N), F32)...  69.7 us
    unnamed x7, local copies, waits for them, and re-layouts  2.71 us

profile of v2, /device:TPU:1, one launch (start us, length us, event | category | flops | bytes accessed | tf_op | source)
XLA Modules:
  0.0 73.1 jit_solution(2669145051804025619)
XLA Ops:
  0.6 69.7 %shard_map.184 = (f32[2,32,512]{2,1,0:T(8,128)}, f32[64,64]{1,0:T(8,128)}, f32[1,64]{1,0:T(1,128)}) custom-call(f32[64,512]{1,0:T(8,128)} %bitcast.4, f32[32,512]{1,0:T(8,128)} %driving.1, f32[64,64]{1,0:T(8,128)} %mixing.1, s32[16,128]{1,0:T(8,128)} %bitcast.5, f32[16,128]{1,0:T(8,128)} %bitcast.6, bf16[160,1024]{1,0:T(8,128)(2,1)} %constant.24.clone.rest_0_, ...), custom_call_target="tpu_custom_call" | custom-call | tf_op jit(solution)/shard_map/pallas_call | solution.py:521
  70.3 0.0 copy-start
  70.4 1.6 %copy.23 = f32[2,32,512]{2,1,0:T(8,128)} copy(f32[2,32,512]{2,1,0:T(8,128)} %get-tuple-element.12) | data formatting | bytes 262144
  71.9 0.0 copy-done
  71.9 0.0 copy-start.1
  71.9 0.6 copy.24
  72.5 0.0 copy-done.1
  72.6 0.5 copy.25
Async XLA Ops:
  70.3 1.6 %copy-start = (f32[64,64]{1,0:T(8,128)S(1)}, f32[64,64]{1,0:T(8,128)}, u32[]{:S(2)}) copy-start(f32[64,64]{1,0:T(8,128)} %get-tuple-element.13) | copy-start | bytes 49156
  71.9 0.6 copy-start.1

commit v3 on v2

--- a/solution.py
+++ b/solution.py
@@ -20,7 +20,6 @@
 GS = 16
 W = KEEP // GS
 QP = 384
-SWAP = True
 
 F32 = jnp.float32
 BF16 = jnp.bfloat16
@@ -76,11 +75,33 @@
 
 
 def swap(m, s):
-    if not SWAP:
-        return m, s
     z_lo, y, core = lax.div(m, 16), lax.rem(lax.div(m, 2), 8), lax.rem(m, 2)
     x, z_hi = lax.div(s, 4), lax.rem(s, 4)
     return lax.div(z_hi, 2) * 16 + y * 2 + lax.rem(z_hi, 2), x * 4 + z_lo * 2 + core
+
+
+def far_first(k):
+    return jnp.where(k == 0, 2, jnp.where(k == 3, 0, 2 * k - 1))
+
+
+def far_first_of_eight(k):
+    return jnp.where(lax.rem(k, 2) == 0, 4 + lax.div(k, 2), 4 - lax.div(k + 1, 2))
+
+
+def space_peer(vs, i):
+    x, z_lo, core = lax.div(vs, 4), lax.rem(lax.div(vs, 2), 2), lax.rem(vs, 2)
+    k, near = lax.div(i, 4), lax.rem(i, 4)
+    x = lax.rem(x + far_first(k), 4)
+    z_lo = lax.rem(z_lo + 1 - lax.div(near, 2), 2)
+    core = lax.rem(core + 1 - lax.rem(near, 2), 2)
+    return x * 4 + z_lo * 2 + core
+
+
+def member_peer(vm, i):
+    z_hi, y = lax.div(vm, 16) * 2 + lax.rem(vm, 2), lax.rem(lax.div(vm, 2), 8)
+    y = lax.rem(y + far_first_of_eight(lax.div(i, 4)), 8)
+    z_hi = lax.rem(z_hi + far_first(lax.rem(i, 4)), 4)
+    return lax.div(z_hi, 2) * 16 + y * 2 + lax.rem(z_hi, 2)
 
 
 def lane_group(shape):
@@ -139,16 +160,16 @@
     swirls, driving, mixing, probes, observed, *rest
 ):
     tables_hbm = rest[:12]
-    analysis, spread, projection = rest[12:15]
+    rows_out, sums_out = rest[12:14]
     (
         f_v, drive_in, drive, mix_v, probes_v, obs_v,
         *more
-    ) = rest[15:]
+    ) = rest[14:]
     tables = more[:12]
     (
         send1, recv1, send2, recv2, send3, recv3, send4, recv4, send5, recv5, send6, recv6,
         hist_s, hist_r, send_a, recv_a, send_b, recv_b, send_c, recv_c,
-        spectrum, members_v, mixed_v,
+        spectrum, members_v, mixed_v, by_row, by_member,
         load_sem, table_sem, send_sem, recv_sem,
     ) = more[12:]
     m, s = lax.axis_index("member"), lax.axis_index("space")
@@ -162,30 +183,27 @@
     def hello(target):
         pl.semaphore_signal(barrier, inc=1, **there(target))
 
-    greeted = (GS - 1) + (GM - 1)
-
-    @pl.loop(1, GS)
-    def _(d):
-        hello(swap(vm, lax.rem(vs + d, GS)))
-
-    @pl.loop(1, GM)
-    def _(d):
-        hello(swap(lax.rem(vm + d, GM), vs))
-
-    if SWAP:
-        @pl.loop(0, GS)
-        def _(p):
-            @pl.when(jnp.logical_or(vm != m, p != s))
-            def _():
-                hello((vm, p))
-
-        @pl.loop(0, GM)
-        def _(a):
-            @pl.when(jnp.logical_or(vs != s, a != vm))
-            def _():
-                hello(swap(a, s))
-
-        greeted = greeted + GS + GM - (vm == m).astype(jnp.int32) - (vs == s).astype(jnp.int32)
+    @pl.loop(0, GS)
+    def _(p):
+        @pl.when(jnp.logical_or(vm != m, p != s))
+        def _():
+            hello((vm, p))
+
+    @pl.loop(0, GS - 1)
+    def _(i):
+        hello(swap(vm, space_peer(vs, i)))
+
+    @pl.loop(0, GM - 1)
+    def _(i):
+        hello(swap(member_peer(vm, i), vs))
+
+    @pl.loop(0, GM)
+    def _(a):
+        @pl.when(jnp.logical_or(vs != s, a != vm))
+        def _():
+            hello(swap(a, s))
+
+    greeted = 2 * (GS + GM - 1) - (vm == m).astype(jnp.int32) - (vs == s).astype(jnp.int32)
 
     loads = [
         pltpu.make_async_copy(src, dst, load_sem.at[i])
@@ -205,26 +223,26 @@
     for copy in table_loads[2:]:
         copy.start()
 
-    pending = []
-
     def copy_out(k, src, dst, target):
         return pltpu.make_async_remote_copy(
             src_ref=src, dst_ref=dst, send_sem=send_sem.at[k], recv_sem=recv_sem.at[k], **there(target)
         )
 
-    def exchange(k, src, dst, axis, many=True):
-        n = GS if axis == "space" else GM
-        me = vs if axis == "space" else vm
+    def exchange(k, src, dst, axis):
+        space = axis == "space"
+        me = vs if space else vm
+
+        @pl.loop(0, (GS if space else GM) - 1)
+        def _(i):
+            p = space_peer(vs, i) if space else member_peer(vm, i)
+            copy_out(k, src(p), dst(me), swap(vm, p) if space else swap(p, vs)).start()
+
         pltpu.make_async_copy(src(me), dst(me), recv_sem.at[k]).start()
 
-        @pl.loop(1, n)
-        def _(d):
-            p = lax.rem(me + d, n)
-            copy_out(k, src(p), dst(me), swap(vm, p) if axis == "space" else swap(p, vs)).start()
-
-    def scatter(k, n, src, dst, target, is_self):
+    def scatter(k, n, order, src, dst, target, is_self):
         @pl.loop(0, n)
-        def _(p):
+        def _(i):
+            p = order(i)
             mine = is_self(p)
 
             @pl.when(mine)
@@ -257,24 +275,22 @@
     send1[...] = out[:, :128] + out[:, 128:] + dot(tables[1][...], rhs_high, NT)
 
     pl.semaphore_wait(barrier, greeted)
-    if SWAP:
-        scatter(
-            0, GS, rows_of(send1, W), recv1.at[pl.ds(W * s, W)], lambda p: swap(m, p),
-            lambda p: jnp.logical_and(vm == m, p == vs),
-        )
-    else:
-        exchange(0, rows_of(send1, W), rows_of(recv1, W), "space")
+    scatter(
+        0, GS, lambda i: space_peer(vs, i), rows_of(send1, W), recv1.at[pl.ds(W * s, W)],
+        lambda p: swap(m, p), lambda p: jnp.logical_and(vm == m, p == vs),
+    )
 
     for copy in loads[1:]:
         copy.wait()
-    if SWAP:
-        @pl.when(jnp.logical_and(vm == m, vs == s))
-        def _():
-            pltpu.make_async_copy(drive_in, drive, recv_sem.at[10]).start()
-
-        @pl.when(jnp.logical_or(vm != m, vs != s))
-        def _():
-            copy_out(10, drive_in, drive, (vm, vs)).start()
+
+    @pl.when(jnp.logical_and(vm == m, vs == s))
+    def _():
+        pltpu.make_async_copy(drive_in, drive, recv_sem.at[10]).start()
+
+    @pl.when(jnp.logical_or(vm != m, vs != s))
+    def _():
+        copy_out(10, drive_in, drive, (vm, vs)).start()
+
     tail = pl.ds(KEEP, 8)
     recv1[tail, :] = jnp.zeros((8, 128), F32)
     recv3[tail, :] = jnp.zeros((8, 128), F32)
@@ -297,14 +313,15 @@
     for i in range(4):
         hist_s[i : i + 1, :] = total[0:1, 128 * i : 128 * i + 128]
         hist_s[4 + i : 5 + i, :] = sums[:, 128 * i : 128 * i + 128]
-    if SWAP:
-        @pl.when(jnp.logical_and(vm == m, vs == s))
-        def _():
-            pltpu.make_async_copy(hist_s, hist_r, recv_sem.at[11]).start()
-
-        @pl.when(jnp.logical_or(vm != m, vs != s))
-        def _():
-            copy_out(11, hist_s, hist_r, (vm, vs)).start()
+
+    @pl.when(jnp.logical_and(vm == m, vs == s))
+    def _():
+        pltpu.make_async_copy(hist_s, hist_r, recv_sem.at[11]).start()
+
+    @pl.when(jnp.logical_or(vm != m, vs != s))
+    def _():
+        copy_out(11, hist_s, hist_r, (vm, vs)).start()
+
     weights = mix_v[...]
     weights = weights + (1.0 - jnp.sum(weights, 0, keepdims=True)) * (1.0 / MEMBERS)
     weights = weights.T
@@ -379,15 +396,11 @@
             send4[pl.ds(W * (4 * hi + slot_), W), :] = got[16 * hi : 16 * hi + W]
     exchange(4, rows_of(send4, W), rows_of(recv4, W), "space")
 
-    if SWAP:
-        finish(10, drive)
-        finish(11, hist_r)
-        drive_ref, hist = drive, hist_r
-    else:
-        drive_ref, hist = drive_in, hist_s
-    forcing = DT_STEP * drive_ref[...]
-    counts = jnp.concatenate([hist[i : i + 1, :] for i in range(4)], 1)
-    obs_sums = jnp.concatenate([hist[4 + i : 5 + i, :] for i in range(4)], 1)
+    finish(10, drive)
+    finish(11, hist_r)
+    forcing = DT_STEP * drive[...]
+    counts = jnp.concatenate([hist_r[i : i + 1, :] for i in range(4)], 1)
+    obs_sums = jnp.concatenate([hist_r[4 + i : 5 + i, :] for i in range(4)], 1)
 
     finish(4, recv4)
     modes = recv4[...].T
@@ -396,16 +409,17 @@
     out = out + dot(jnp.concatenate([high[64:], low[64:]], 0), tables[10][...])
     fresh = out[:64] + out[64:] + dot(high[:64], tables[9][...]) + dot(high[64:], tables[11][...])
     fresh = fresh + jnp.concatenate([forcing, forcing], 0)
-    rounded = fresh.astype(BF16).astype(F32)
     for k in range(2):
         for i in range(4):
-            send5[:, 4 * k + i, :] = rounded[32 * k : 32 * k + 32, 128 * i : 128 * i + 128]
+            by_row[:, 4 * k + i, :] = fresh[32 * k : 32 * k + 32, 128 * i : 128 * i + 128]
+    send5[...] = by_row[...].astype(BF16)
     exchange(5, lambda p: send5.at[p], lambda p: recv5.at[p], "member")
 
     finish(5, recv5)
+    by_member[...] = recv5[...].astype(F32)
     for k in range(2):
         for i in range(4):
-            members_v[i, pl.ds(k, 32, stride=2), :] = recv5[:, 4 * k + i, :]
+            members_v[i, pl.ds(k, 32, stride=2), :] = by_member[:, 4 * k + i, :]
     values = jnp.concatenate([members_v[i] for i in range(4)], 1)
 
     centre = jnp.sum(values, 0, keepdims=True) * (1.0 / MEMBERS)
@@ -426,14 +440,6 @@
     for k in range(2):
         for i in range(4):
             send6[:, 4 * k + i, :] = mixed_v[i, pl.ds(k, 32, stride=2), :]
-    if SWAP:
-        scatter(
-            6, GM, lambda p: send6.at[p], recv6.at[vm], lambda p: (p, vs),
-            lambda p: jnp.logical_and(vs == s, p == m),
-        )
-    else:
-        exchange(6, lambda p: send6.at[p], lambda p: recv6.at[p], "member")
-
     finish(7, recv_a)
     chunk = recv_a[pl.ds(0, 4), :]
     for p in range(1, GS):
@@ -441,10 +447,10 @@
     send_b[...] = chunk
     exchange(8, lambda p: send_b, rows_of(recv_b, 4), "member")
 
-    finish(6, recv6)
-    for k in range(2):
-        for i in range(4):
-            analysis[k, :, pl.ds(128 * i, 128)] = recv6[:, 4 * k + i, :]
+    scatter(
+        6, GM, lambda i: member_peer(vm, i), lambda p: send6.at[p], recv6.at[vm],
+        lambda p: (p, vs), lambda p: jnp.logical_and(vs == s, p == m),
+    )
 
     finish(8, recv_b)
     chunk = recv_b[pl.ds(0, 4), :]
@@ -452,13 +458,11 @@
         chunk = chunk + recv_b[pl.ds(4 * p, 4), :]
     send_c[...] = chunk
     exchange(9, lambda p: send_c, rows_of(recv_c, 4), "space")
+    finish(6, recv6)
+    rows_out[...] = recv6[...]
+
     finish(9, recv_c)
-    full = recv_c[...]
-    spread[...] = full[:, :64] * (1.0 / PROBES)
-    shape = (64, 64)
-    diagonal = lax.broadcasted_iota(jnp.int32, shape, 0) == lax.broadcasted_iota(jnp.int32, shape, 1)
-    column = jnp.where(diagonal, full[:, 64:65], 0.0)
-    projection[...] = jnp.sum(column, 0, keepdims=True) * (1.0 / math.sqrt(PROBES))
+    sums_out[...] = recv_c[...]
 
     others = {
         0: send1.at[pl.ds(0, W * (GS - 1))],
@@ -478,19 +482,31 @@
 
     for k, ref in others.items():
         sent(k, ref)
-    if SWAP:
-        @pl.when(vm != m)
-        def _():
-            sent(0, send1.at[pl.ds(0, W)])
-
-        @pl.when(vs != s)
-        def _():
-            sent(6, send6.at[0])
-
-        @pl.when(jnp.logical_or(vm != m, vs != s))
-        def _():
-            sent(10, drive_in)
-            sent(11, hist_s)
+
+    @pl.when(vm != m)
+    def _():
+        sent(0, send1.at[pl.ds(0, W)])
+
+    @pl.when(vs != s)
+    def _():
+        sent(6, send6.at[0])
+
+    @pl.when(jnp.logical_or(vm != m, vs != s))
+    def _():
+        sent(10, drive_in)
+        sent(11, hist_s)
+
+
+def finish_kernel(rows, sums, analysis, spread, projection):
+    for k in range(2):
+        for i in range(4):
+            analysis[k, :, pl.ds(128 * i, 128)] = rows[:, 4 * k + i, :]
+    full = sums[...]
+    spread[...] = full[:, :64] * (1.0 / PROBES)
+    shape = (64, 64)
+    diagonal = lax.broadcasted_iota(jnp.int32, shape, 0) == lax.broadcasted_iota(jnp.int32, shape, 1)
+    column = jnp.where(diagonal, full[:, 64:65], 0.0)
+    projection[...] = jnp.sum(column, 0, keepdims=True) * (1.0 / math.sqrt(PROBES))
 
 
 def on_device(swirls, driving, mixing, probes, observed):
@@ -509,24 +525,24 @@
         (2, 2 * KEEP, lanes), (2, 2 * KEEP, lanes),
         (KEEP, lanes), (KEEP + 8, lanes),
         (KEEP, lanes), (KEEP, lanes),
-        (GM, 8, lanes), (GM, 8, lanes), (GM, 8, lanes), (GM, 8, lanes),
+        (GM, 8, lanes, BF16), (GM, 8, lanes, BF16), (GM, 8, lanes), (GM, 8, lanes),
         (8, lanes), (8, lanes),
         (64, lanes), (64, lanes), (4, lanes), (4 * GM, lanes), (4, lanes), (64, lanes),
-        (64, QP), (4, 64, lanes), (4, 64, lanes),
+        (64, QP), (4, 64, lanes), (4, 64, lanes), (GM, 8, lanes), (GM, 8, lanes),
     ]:
-        scratch.append(vmem(shape, F32))
+        narrow = shape[-1] is BF16
+        scratch.append(vmem(shape[:-1], BF16) if narrow else vmem(shape, F32))
     dma = pltpu.SemaphoreType.DMA
     scratch += [dma((5,)), dma((12,)), dma((12,)), dma((12,))]
     anywhere = pl.BlockSpec(memory_space=pl.ANY)
-    analysis, spread, projection = pl.pallas_call(
+    rows, sums = pl.pallas_call(
         kernel,
         out_shape=[
-            jax.ShapeDtypeStruct((2, ROWS, N), F32),
-            jax.ShapeDtypeStruct((64, 64), F32),
-            jax.ShapeDtypeStruct((1, 64), F32),
+            jax.ShapeDtypeStruct((GM, 8, lanes), F32),
+            jax.ShapeDtypeStruct((64, lanes), F32),
         ],
         in_specs=[anywhere] * (5 + len(tables)),
-        out_specs=[pl.BlockSpec(memory_space=pltpu.VMEM)] * 3,
+        out_specs=[pl.BlockSpec(memory_space=pltpu.VMEM)] * 2,
         scratch_shapes=scratch,
         compiler_params=pltpu.CompilerParams(
             collective_id=0, has_side_effects=True, vmem_limit_bytes=60 * 2**20
@@ -535,6 +551,16 @@
         swirls.reshape(64, N), driving, mixing, probes.reshape(16, 128), observed.reshape(16, 128),
         *tables,
     )
+    analysis, spread, projection = pl.pallas_call(
+        finish_kernel,
+        out_shape=[
+            jax.ShapeDtypeStruct((2, ROWS, N), F32),
+            jax.ShapeDtypeStruct((64, 64), F32),
+            jax.ShapeDtypeStruct((1, 64), F32),
+        ],
+        in_specs=[pl.BlockSpec(memory_space=pltpu.VMEM)] * 2,
+        out_specs=[pl.BlockSpec(memory_space=pltpu.VMEM)] * 3,
+    )(rows, sums)
     return analysis, spread, projection.reshape(64)
 
 

time: 73.2 us -> 68.4 us (0.934)
  local copies, waits for them, and re-layouts: 2.71 us -> 0 us
  Pallas kernels: 69.7 us -> 67.6 us
    unnamed x7 -> x0, local copies, waits for them, and re-layouts: 2.71 us -> none
    pallas_call x1 -> x2, Pallas kernels: 69.7 us -> 67.6 us  [the longest x1 66 us: on_device(): pl.pallas_call(kernel, out_shape=[jax.ShapeDtypeStruct((GM, 8, lanes), F3...]
where the time goes in v3:
time: 68.4 us; the launch traced here: 68.3 us
  Pallas kernels  67.6 us (99%)
    pallas_call x1, Pallas kernels, on_device(): pl.pallas_call(kernel, out_shape=[jax.ShapeDtypeStruct((GM, 8, lanes), F3...  66 us
    pallas_call x1, Pallas kernels, on_device(): pl.pallas_call(finish_kernel, out_shape=[jax.ShapeDtypeStruct((2, ROWS, N...  1.65 us

profile of v3, /device:TPU:1, one launch (start us, length us, event | category | flops | bytes accessed | tf_op | source)
XLA Modules:
  0.0 68.3 jit_solution(2389959014724798531)
XLA Ops:
  0.6 66.0 %shard_map.184 = (f32[32,8,128]{2,1,0:T(8,128)}, f32[64,128]{1,0:T(8,128)}) custom-call(f32[64,512]{1,0:T(8,128)} %bitcast.4, f32[32,512]{1,0:T(8,128)} %driving.1, f32[64,64]{1,0:T(8,128)} %mixing.1, s32[16,128]{1,0:T(8,128)} %bitcast.5, f32[16,128]{1,0:T(8,128)} %bitcast.6, bf16[160,1024]{1,0:T(8,128)(2,1)} %constant.24.clone.rest_0_, ...), custom_call_target="tpu_custom_call" | custom-call | tf_op jit(solution)/shard_map/pallas_call | solution.py:538
  66.6 1.7 %shard_map.185 = (f32[2,32,512]{2,1,0:T(8,128)}, f32[64,64]{1,0:T(8,128)}, f32[1,64]{1,0:T(1,128)}) custom-call(f32[32,8,128]{2,1,0:T(8,128)} %get-tuple-element.8.rows, f32[64,128]{1,0:T(8,128)} %get-tuple-element.9.sums), custom_call_target="tpu_custom_call" | custom-call | tf_op jit(solution)/shard_map/pallas_call | solution.py:554

commit v4 on v3

--- a/solution.py
+++ b/solution.py
@@ -74,34 +74,22 @@
     return high, (x - high.astype(F32)).astype(BF16)
 
 
-def swap(m, s):
-    z_lo, y, core = lax.div(m, 16), lax.rem(lax.div(m, 2), 8), lax.rem(m, 2)
-    x, z_hi = lax.div(s, 4), lax.rem(s, 4)
-    return lax.div(z_hi, 2) * 16 + y * 2 + lax.rem(z_hi, 2), x * 4 + z_lo * 2 + core
-
-
-def far_first(k):
-    return jnp.where(k == 0, 2, jnp.where(k == 3, 0, 2 * k - 1))
-
-
-def far_first_of_eight(k):
-    return jnp.where(lax.rem(k, 2) == 0, 4 + lax.div(k, 2), 4 - lax.div(k + 1, 2))
-
-
-def space_peer(vs, i):
-    x, z_lo, core = lax.div(vs, 4), lax.rem(lax.div(vs, 2), 2), lax.rem(vs, 2)
-    k, near = lax.div(i, 4), lax.rem(i, 4)
-    x = lax.rem(x + far_first(k), 4)
-    z_lo = lax.rem(z_lo + 1 - lax.div(near, 2), 2)
-    core = lax.rem(core + 1 - lax.rem(near, 2), 2)
-    return x * 4 + z_lo * 2 + core
-
-
-def member_peer(vm, i):
-    z_hi, y = lax.div(vm, 16) * 2 + lax.rem(vm, 2), lax.rem(lax.div(vm, 2), 8)
-    y = lax.rem(y + far_first_of_eight(lax.div(i, 4)), 8)
-    z_hi = lax.rem(z_hi + far_first(lax.rem(i, 4)), 4)
-    return lax.div(z_hi, 2) * 16 + y * 2 + lax.rem(z_hi, 2)
+def hops(step, ring):
+    return min(step, ring - step)
+
+
+NEAR = sorted(
+    ((dx, a, b) for dx in range(4) for a in range(2) for b in range(2)),
+    key=lambda d: (-hops(d[0], 4) - d[1], -d[2]),
+)
+FAR = sorted(
+    ((dy, dz) for dy in range(8) for dz in range(4)),
+    key=lambda d: (-hops(d[0], 8) - 2 * hops(d[1], 4), -d[0]),
+)
+BACK = sorted(
+    ((dy, a, b) for dy in range(8) for a in range(2) for b in range(2)),
+    key=lambda d: (-hops(d[0], 8), -d[1], -d[2]),
+)
 
 
 def lane_group(shape):
@@ -173,7 +161,35 @@
         load_sem, table_sem, send_sem, recv_sem,
     ) = more[12:]
     m, s = lax.axis_index("member"), lax.axis_index("space")
-    vm, vs = swap(m, s)
+    x, z_hi = lax.div(s, 4), lax.rem(s, 4)
+    z_lo, y, core = lax.div(m, 16), lax.rem(lax.div(m, 2), 8), lax.rem(m, 2)
+    hi_hi, hi_lo = lax.div(z_hi, 2), lax.rem(z_hi, 2)
+    pair = z_lo * 2 + core
+    vm, vs = hi_hi * 16 + y * 2 + hi_lo, x * 4 + pair
+    fixed = z_hi == pair
+    moved = z_hi != pair
+    xs = [x] + [lax.rem(x + d, 4) for d in range(1, 4)]
+    ys = [y] + [lax.rem(y + d, 8) for d in range(1, 8)]
+    zs = [z_hi] + [lax.rem(z_hi + d, 4) for d in range(1, 4)]
+    lows, cores = [z_lo, 1 - z_lo], [core, 1 - core]
+    near_m = {(a, b): lows[a] * 16 + y * 2 + cores[b] for a in range(2) for b in range(2)}
+    back_m = [lows[0] * 16, lows[1] * 16]
+    z_m = [lax.div(z, 2) * 16 + lax.rem(z, 2) for z in zs]
+
+    def near_peer(d):
+        return xs[d[0]] * 4 + lows[d[1]] * 2 + cores[d[2]]
+
+    def near_device(d, z):
+        return near_m[d[1], d[2]], xs[d[0]] * 4 + z
+
+    def far_peer(d):
+        return z_m[d[1]] + ys[d[0]] * 2
+
+    def far_device(d, low, core_):
+        return low * 16 + ys[d[0]] * 2 + core_, x * 4 + zs[d[1]]
+
+    def back_peer(d):
+        return back_m[d[1]] + ys[d[0]] * 2 + cores[d[2]]
 
     def there(target):
         return dict(device_id={"member": target[0], "space": target[1]}, device_id_type=MESH)
@@ -183,27 +199,20 @@
     def hello(target):
         pl.semaphore_signal(barrier, inc=1, **there(target))
 
-    @pl.loop(0, GS)
-    def _(p):
-        @pl.when(jnp.logical_or(vm != m, p != s))
-        def _():
-            hello((vm, p))
-
-    @pl.loop(0, GS - 1)
-    def _(i):
-        hello(swap(vm, space_peer(vs, i)))
-
-    @pl.loop(0, GM - 1)
-    def _(i):
-        hello(swap(member_peer(vm, i), vs))
-
-    @pl.loop(0, GM)
-    def _(a):
-        @pl.when(jnp.logical_or(vs != s, a != vm))
-        def _():
-            hello(swap(a, s))
-
-    greeted = 2 * (GS + GM - 1) - (vm == m).astype(jnp.int32) - (vs == s).astype(jnp.int32)
+    for d in FAR[:-1]:
+        hello(far_device(d, z_lo, core))
+        hello(far_device(d, hi_hi, hi_lo))
+    for dx, dz in [(2, 2), (2, 1), (2, 3), (1, 2), (3, 2), (2, 0), (0, 2), (1, 1), (1, 3), (3, 1), (3, 3), (1, 0), (3, 0), (0, 1), (0, 3)]:
+        hello((vm, xs[dx] * 4 + zs[dz]))
+    for d in NEAR[:-1]:
+        hello(near_device(d, z_hi))
+
+    @pl.when(moved)
+    def _():
+        hello(far_device(FAR[-1], hi_hi, hi_lo))
+        hello((vm, s))
+
+    greeted = 2 * (GS + GM - 2) + 2 * moved.astype(jnp.int32)
 
     loads = [
         pltpu.make_async_copy(src, dst, load_sem.at[i])
@@ -229,29 +238,27 @@
         )
 
     def exchange(k, src, dst, axis):
-        space = axis == "space"
-        me = vs if space else vm
-
-        @pl.loop(0, (GS if space else GM) - 1)
-        def _(i):
-            p = space_peer(vs, i) if space else member_peer(vm, i)
-            copy_out(k, src(p), dst(me), swap(vm, p) if space else swap(p, vs)).start()
-
+        me = vs if axis == "space" else vm
+        for d in NEAR[:-1] if axis == "space" else FAR[:-1]:
+            if axis == "space":
+                p, target = near_peer(d), near_device(d, z_hi)
+            else:
+                p, target = far_peer(d), far_device(d, z_lo, core)
+            copy_out(k, src(p), dst(me), target).start()
         pltpu.make_async_copy(src(me), dst(me), recv_sem.at[k]).start()
 
-    def scatter(k, n, order, src, dst, target, is_self):
-        @pl.loop(0, n)
-        def _(i):
-            p = order(i)
-            mine = is_self(p)
-
-            @pl.when(mine)
-            def _():
-                pltpu.make_async_copy(src(p), dst, recv_sem.at[k]).start()
-
-            @pl.when(jnp.logical_not(mine))
-            def _():
-                copy_out(k, src(p), dst, target(p)).start()
+    def scatter(k, steps, peer, device, src, dst):
+        for d in steps[:-1]:
+            copy_out(k, src(peer(d)), dst, device(d)).start()
+        p = peer(steps[-1])
+
+        @pl.when(fixed)
+        def _():
+            pltpu.make_async_copy(src(p), dst, recv_sem.at[k]).start()
+
+        @pl.when(moved)
+        def _():
+            copy_out(k, src(p), dst, device(steps[-1])).start()
 
     def finish(k, ref):
         pltpu.make_async_copy(ref, ref, recv_sem.at[k]).wait()
@@ -276,18 +283,17 @@
 
     pl.semaphore_wait(barrier, greeted)
     scatter(
-        0, GS, lambda i: space_peer(vs, i), rows_of(send1, W), recv1.at[pl.ds(W * s, W)],
-        lambda p: swap(m, p), lambda p: jnp.logical_and(vm == m, p == vs),
+        0, NEAR, near_peer, lambda d: near_device(d, pair), rows_of(send1, W), recv1.at[pl.ds(W * s, W)]
     )
 
     for copy in loads[1:]:
         copy.wait()
 
-    @pl.when(jnp.logical_and(vm == m, vs == s))
+    @pl.when(fixed)
     def _():
         pltpu.make_async_copy(drive_in, drive, recv_sem.at[10]).start()
 
-    @pl.when(jnp.logical_or(vm != m, vs != s))
+    @pl.when(moved)
     def _():
         copy_out(10, drive_in, drive, (vm, vs)).start()
 
@@ -314,11 +320,11 @@
         hist_s[i : i + 1, :] = total[0:1, 128 * i : 128 * i + 128]
         hist_s[4 + i : 5 + i, :] = sums[:, 128 * i : 128 * i + 128]
 
-    @pl.when(jnp.logical_and(vm == m, vs == s))
+    @pl.when(fixed)
     def _():
         pltpu.make_async_copy(hist_s, hist_r, recv_sem.at[11]).start()
 
-    @pl.when(jnp.logical_or(vm != m, vs != s))
+    @pl.when(moved)
     def _():
         copy_out(11, hist_s, hist_r, (vm, vs)).start()
 
@@ -448,8 +454,7 @@
     exchange(8, lambda p: send_b, rows_of(recv_b, 4), "member")
 
     scatter(
-        6, GM, lambda i: member_peer(vm, i), lambda p: send6.at[p], recv6.at[vm],
-        lambda p: (p, vs), lambda p: jnp.logical_and(vs == s, p == m),
+        6, BACK, back_peer, lambda d: (back_peer(d), vs), lambda p: send6.at[p], recv6.at[vm]
     )
 
     finish(8, recv_b)
@@ -483,15 +488,15 @@
     for k, ref in others.items():
         sent(k, ref)
 
-    @pl.when(vm != m)
+    @pl.when(moved)
     def _():
         sent(0, send1.at[pl.ds(0, W)])
 
-    @pl.when(vs != s)
+    @pl.when(moved)
     def _():
         sent(6, send6.at[0])
 
-    @pl.when(jnp.logical_or(vm != m, vs != s))
+    @pl.when(moved)
     def _():
         sent(10, drive_in)
         sent(11, hist_s)

time: 68.4 us -> 66.5 us (0.972)
  Pallas kernels: 67.6 us -> 65.7 us
    pallas_call x1, Pallas kernels: 66 us -> 64 us  [on_device(): pl.pallas_call(kernel, out_shape=[jax.ShapeDtypeStruct((GM, 8, lanes), F3...]
where the time goes in v4:
time: 66.5 us; the launch traced here: 66.3 us
  Pallas kernels  65.7 us (99%)
    pallas_call x1, Pallas kernels, on_device(): pl.pallas_call(kernel, out_shape=[jax.ShapeDtypeStruct((GM, 8, lanes), F3...  64 us
    pallas_call x1, Pallas kernels, on_device(): pl.pallas_call(finish_kernel, out_shape=[jax.ShapeDtypeStruct((2, ROWS, N...  1.65 us

profile of v4, /device:TPU:1, one launch (start us, length us, event | category | flops | bytes accessed | tf_op | source)
XLA Modules:
  0.0 66.3 jit_solution(5083556941683620955)
XLA Ops:
  0.6 64.0 %shard_map.184 = (f32[32,8,128]{2,1,0:T(8,128)}, f32[64,128]{1,0:T(8,128)}) custom-call(f32[64,512]{1,0:T(8,128)} %bitcast.4, f32[32,512]{1,0:T(8,128)} %driving.1, f32[64,64]{1,0:T(8,128)} %mixing.1, s32[16,128]{1,0:T(8,128)} %bitcast.5, f32[16,128]{1,0:T(8,128)} %bitcast.6, bf16[160,1024]{1,0:T(8,128)(2,1)} %constant.24.clone.rest_0_, ...), custom_call_target="tpu_custom_call" | custom-call | tf_op jit(solution)/shard_map/pallas_call | solution.py:543
  64.7 1.7 %shard_map.185 = (f32[2,32,512]{2,1,0:T(8,128)}, f32[64,64]{1,0:T(8,128)}, f32[1,64]{1,0:T(1,128)}) custom-call(f32[32,8,128]{2,1,0:T(8,128)} %get-tuple-element.8.rows, f32[64,128]{1,0:T(8,128)} %get-tuple-element.9.sums), custom_call_target="tpu_custom_call" | custom-call | tf_op jit(solution)/shard_map/pallas_call | solution.py:559

commit v5 on v4

--- a/solution.py
+++ b/solution.py
@@ -158,7 +158,7 @@
         send1, recv1, send2, recv2, send3, recv3, send4, recv4, send5, recv5, send6, recv6,
         hist_s, hist_r, send_a, recv_a, send_b, recv_b, send_c, recv_c,
         spectrum, members_v, mixed_v, by_row, by_member,
-        load_sem, table_sem, send_sem, recv_sem,
+        load_sem, table_sem, send_sem, recv_sem, store_sem,
     ) = more[12:]
     m, s = lax.axis_index("member"), lax.axis_index("space")
     x, z_hi = lax.div(s, 4), lax.rem(s, 4)
@@ -288,15 +288,6 @@
 
     for copy in loads[1:]:
         copy.wait()
-
-    @pl.when(fixed)
-    def _():
-        pltpu.make_async_copy(drive_in, drive, recv_sem.at[10]).start()
-
-    @pl.when(moved)
-    def _():
-        copy_out(10, drive_in, drive, (vm, vs)).start()
-
     tail = pl.ds(KEEP, 8)
     recv1[tail, :] = jnp.zeros((8, 128), F32)
     recv3[tail, :] = jnp.zeros((8, 128), F32)
@@ -319,15 +310,6 @@
     for i in range(4):
         hist_s[i : i + 1, :] = total[0:1, 128 * i : 128 * i + 128]
         hist_s[4 + i : 5 + i, :] = sums[:, 128 * i : 128 * i + 128]
-
-    @pl.when(fixed)
-    def _():
-        pltpu.make_async_copy(hist_s, hist_r, recv_sem.at[11]).start()
-
-    @pl.when(moved)
-    def _():
-        copy_out(11, hist_s, hist_r, (vm, vs)).start()
-
     weights = mix_v[...]
     weights = weights + (1.0 - jnp.sum(weights, 0, keepdims=True)) * (1.0 / MEMBERS)
     weights = weights.T
@@ -387,6 +369,22 @@
     send3[...] = out[:, :128] + out[:, 128:] + dot(tables[1][...], high)
     exchange(3, rows_of(send3, W), rows_of(recv3, W), "space")
 
+    @pl.when(fixed)
+    def _():
+        pltpu.make_async_copy(drive_in, drive, recv_sem.at[10]).start()
+
+    @pl.when(moved)
+    def _():
+        copy_out(10, drive_in, drive, (vm, vs)).start()
+
+    @pl.when(fixed)
+    def _():
+        pltpu.make_async_copy(hist_s, hist_r, recv_sem.at[11]).start()
+
+    @pl.when(moved)
+    def _():
+        copy_out(11, hist_s, hist_r, (vm, vs)).start()
+
     finish(3, recv3.at[pl.ds(0, KEEP)])
     adv = to_slots(gather_columns(recv3), tables[2][...], tables[3][...])
     w = spectrum[...]
@@ -464,10 +462,20 @@
     send_c[...] = chunk
     exchange(9, lambda p: send_c, rows_of(recv_c, 4), "space")
     finish(6, recv6)
-    rows_out[...] = recv6[...]
+    stores = [
+        pltpu.make_async_copy(
+            recv6.at[:, 4 * k + i, :], rows_out.at[k, :, pl.ds(128 * i, 128)], store_sem.at[4 * k + i]
+        )
+        for k in range(2) for i in range(4)
+    ]
+    for copy in stores:
+        copy.start()
 
     finish(9, recv_c)
     sums_out[...] = recv_c[...]
+
+    for copy in stores:
+        copy.wait()
 
     others = {
         0: send1.at[pl.ds(0, W * (GS - 1))],
@@ -503,9 +511,7 @@
 
 
 def finish_kernel(rows, sums, analysis, spread, projection):
-    for k in range(2):
-        for i in range(4):
-            analysis[k, :, pl.ds(128 * i, 128)] = rows[:, 4 * k + i, :]
+    analysis[...] = rows[...]
     full = sums[...]
     spread[...] = full[:, :64] * (1.0 / PROBES)
     shape = (64, 64)
@@ -538,16 +544,16 @@
         narrow = shape[-1] is BF16
         scratch.append(vmem(shape[:-1], BF16) if narrow else vmem(shape, F32))
     dma = pltpu.SemaphoreType.DMA
-    scratch += [dma((5,)), dma((12,)), dma((12,)), dma((12,))]
+    scratch += [dma((5,)), dma((12,)), dma((12,)), dma((12,)), dma((8,))]
     anywhere = pl.BlockSpec(memory_space=pl.ANY)
     rows, sums = pl.pallas_call(
         kernel,
         out_shape=[
-            jax.ShapeDtypeStruct((GM, 8, lanes), F32),
+            jax.ShapeDtypeStruct((2, ROWS, N), F32),
             jax.ShapeDtypeStruct((64, lanes), F32),
         ],
         in_specs=[anywhere] * (5 + len(tables)),
-        out_specs=[pl.BlockSpec(memory_space=pltpu.VMEM)] * 2,
+        out_specs=[anywhere, pl.BlockSpec(memory_space=pltpu.VMEM)],
         scratch_shapes=scratch,
         compiler_params=pltpu.CompilerParams(
             collective_id=0, has_side_effects=True, vmem_limit_bytes=60 * 2**20
@@ -565,6 +571,7 @@
         ],
         in_specs=[pl.BlockSpec(memory_space=pltpu.VMEM)] * 2,
         out_specs=[pl.BlockSpec(memory_space=pltpu.VMEM)] * 3,
+        compiler_params=pltpu.CompilerParams(vmem_limit_bytes=60 * 2**20),
     )(rows, sums)
     return analysis, spread, projection.reshape(64)
 

time: 66.5 us -> 66.2 us (level)
  no operation moved by 1% of the time
where the time goes in v5:
time: 66.2 us; the launch traced here: 66.1 us
  Pallas kernels  65.5 us (99%)
    pallas_call x1, Pallas kernels, on_device(): pl.pallas_call(kernel, out_shape=[jax.ShapeDtypeStruct((2, ROWS, N), F32)...  63.9 us
    pallas_call x1, Pallas kernels, on_device(): pl.pallas_call(finish_kernel, out_shape=[jax.ShapeDtypeStruct((2, ROWS, N...  1.58 us

profile of v5, /device:TPU:1, one launch (start us, length us, event | category | flops | bytes accessed | tf_op | source)
XLA Modules:
  0.0 66.1 jit_solution(8252482529854557344)
XLA Ops:
  0.6 63.9 %shard_map.184 = (f32[2,32,512]{2,1,0:T(8,128)}, f32[64,128]{1,0:T(8,128)}) custom-call(f32[64,512]{1,0:T(8,128)} %bitcast.4, f32[32,512]{1,0:T(8,128)} %driving.1, f32[64,64]{1,0:T(8,128)} %mixing.1, s32[16,128]{1,0:T(8,128)} %bitcast.5, f32[16,128]{1,0:T(8,128)} %bitcast.6, bf16[160,1024]{1,0:T(8,128)(2,1)} %constant.24.clone.rest_0_, ...), custom_call_target="tpu_custom_call" | custom-call | tf_op jit(solution)/shard_map/pallas_call | solution.py:549
  64.5 1.6 %shard_map.185 = (f32[2,32,512]{2,1,0:T(8,128)}, f32[64,64]{1,0:T(8,128)}, f32[1,64]{1,0:T(1,128)}) custom-call(f32[2,32,512]{2,1,0:T(8,128)} %get-tuple-element.8.rows, f32[64,128]{1,0:T(8,128)} %get-tuple-element.9.sums), custom_call_target="tpu_custom_call" | custom-call | tf_op jit(solution)/shard_map/pallas_call | solution.py:565

commit v6 on v5

--- a/solution.py
+++ b/solution.py
@@ -444,16 +444,16 @@
     for k in range(2):
         for i in range(4):
             send6[:, 4 * k + i, :] = mixed_v[i, pl.ds(k, 32, stride=2), :]
+    scatter(
+        6, BACK, back_peer, lambda d: (back_peer(d), vs), lambda p: send6.at[p], recv6.at[vm]
+    )
+
     finish(7, recv_a)
     chunk = recv_a[pl.ds(0, 4), :]
     for p in range(1, GS):
         chunk = chunk + recv_a[pl.ds(4 * p, 4), :]
     send_b[...] = chunk
     exchange(8, lambda p: send_b, rows_of(recv_b, 4), "member")
-
-    scatter(
-        6, BACK, back_peer, lambda d: (back_peer(d), vs), lambda p: send6.at[p], recv6.at[vm]
-    )
 
     finish(8, recv_b)
     chunk = recv_b[pl.ds(0, 4), :]

time: 66.2 us -> 67 us (1.012)
  Pallas kernels: 65.5 us -> 66.3 us
    pallas_call x1, Pallas kernels: 63.9 us -> 64.7 us  [on_device(): pl.pallas_call(kernel, out_shape=[jax.ShapeDtypeStruct((2, ROWS, N), F32)...]
where the time goes in v6:
time: 67 us; the launch traced here: 66.9 us
  Pallas kernels  66.3 us (99%)
    pallas_call x1, Pallas kernels, on_device(): pl.pallas_call(kernel, out_shape=[jax.ShapeDtypeStruct((2, ROWS, N), F32)...  64.7 us
    pallas_call x1, Pallas kernels, on_device(): pl.pallas_call(finish_kernel, out_shape=[jax.ShapeDtypeStruct((2, ROWS, N...  1.58 us

profile of v6, /device:TPU:1, one launch (start us, length us, event | category | flops | bytes accessed | tf_op | source)
XLA Modules:
  0.0 66.9 jit_solution(15385764767831180479)
XLA Ops:
  0.6 64.7 %shard_map.184 = (f32[2,32,512]{2,1,0:T(8,128)}, f32[64,128]{1,0:T(8,128)}) custom-call(f32[64,512]{1,0:T(8,128)} %bitcast.4, f32[32,512]{1,0:T(8,128)} %driving.1, f32[64,64]{1,0:T(8,128)} %mixing.1, s32[16,128]{1,0:T(8,128)} %bitcast.5, f32[16,128]{1,0:T(8,128)} %bitcast.6, bf16[160,1024]{1,0:T(8,128)(2,1)} %constant.24.clone.rest_0_, ...), custom_call_target="tpu_custom_call" | custom-call | tf_op jit(solution)/shard_map/pallas_call | solution.py:549
  65.3 1.6 %shard_map.185 = (f32[2,32,512]{2,1,0:T(8,128)}, f32[64,64]{1,0:T(8,128)}, f32[1,64]{1,0:T(1,128)}) custom-call(f32[2,32,512]{2,1,0:T(8,128)} %get-tuple-element.8.rows, f32[64,128]{1,0:T(8,128)} %get-tuple-element.9.sums), custom_call_target="tpu_custom_call" | custom-call | tf_op jit(solution)/shard_map/pallas_call | solution.py:565
